TPU v7x, 768 devices: a whole 4x8x12 slice. The times are simulated.
768 devices in a mesh: mem: 32 (over y, x), patch: 24 (over z, core).
Axes of the slice: x: 4, y: 8, z: 12, core: 2. Of those that a mesh axis runs over, the one named last changes fastest.
Arguments:
- state: bfloat16 [1024, 393216], P('mem', 'patch'), may hold values from -6 to 6
- obs_ens: bfloat16 [1024, 196608], P('mem', 'patch'), may hold values from -6 to 6
- obs_values: float32 [196608], P('patch'), may hold values from -8 to 8
- obs_weight: float32 [196608], P('patch'), may hold values from 0.2 to 5
- counts: int32 [768], P('patch'), may hold values from 32 to 256
Outputs:
- analysis: bfloat16 [1024, 393216], P('mem', 'patch')
Inputs may be any that keep to these rules, and one draw needn't show every extreme that they name: Region r uses the first counts[r] of its 256 observations.
All inputs are finite; a program needn't handle non-finite values. Where the computation divides by a largest or mean magnitude, that divisor is 1e-20 or more.
Results may differ from a plain program's by a relative error of at most 0.0047.
Values may be sent and summed in bfloat16 or wider, within the bound.
No kernel may reach another device: no remote copies, remote signals or barrier semaphores. Data moves between devices by JAX's collectives and lax.ppermute only.
A program may use at most 32 MiB of HBM per device.

v0:
```python
import math

import jax
import jax.numpy as jnp
from jax import lax
from jax.sharding import PartitionSpec as P

DEGREE = 7


def extended(cells, sides, width):
    for axis, dim in sides:
        count = lax.axis_size(axis)
        head = lax.slice_in_dim(cells, 0, width, axis=dim)
        tail = lax.slice_in_dim(cells, cells.shape[dim] - width, cells.shape[dim], axis=dim)
        cells = jnp.concatenate(
            [
                lax.ppermute(tail, axis, [(i, (i + 1) % count) for i in range(count)]),
                cells,
                lax.ppermute(head, axis, [((i + 1) % count, i) for i in range(count)]),
            ],
            axis=dim,
        )
    return cells


def root_curve(values):
    lifted = jnp.sqrt(1.0 + values)
    return -1.0 / (lifted * (1.0 + lifted))


def inverse_curve(values):
    return 1.0 / (1.0 + values)


def chebyshev(upper, curve):
    number = DEGREE + 1
    theta = (jnp.arange(number, dtype=jnp.float32) + 0.5) * (math.pi / number)
    nodes = upper * (jnp.cos(theta) + 1.0) * 0.5
    samples = curve(nodes)
    orders = jnp.arange(number, dtype=jnp.float32)
    table = jnp.cos(orders[:, None] * theta[None, :])
    coefs = 2.0 / number * jnp.sum(table * samples[None, :], axis=1)
    return coefs * jnp.where(orders == 0.0, 0.5, 1.0)


def clenshaw(block, matrix, coefs):
    nearer = coefs[DEGREE] * block
    farther = jnp.zeros_like(block)
    for order in range(DEGREE - 1, 0, -1):
        current = (
            coefs[order] * block
            + 2.0 * jnp.dot(nearer, matrix, precision=lax.Precision.HIGHEST)
            - farther
        )
        farther, nearer = (nearer, current)
    return coefs[0] * block + jnp.dot(nearer, matrix, precision=lax.Precision.HIGHEST) - farther


def cross_product(left, right):
    return lax.dot_general(
        left, right, (((0,), (0,)), ((), ())), preferred_element_type=jnp.float32
    )


def on_device(state, obs_ens, obs_values, obs_weight, counts):
    mem_index = lax.axis_index("mem")
    own = obs_ens.shape[1] // lax.axis_size("mem")
    half = own // 2
    values = lax.dynamic_slice_in_dim(obs_values, mem_index * own, own, 0)
    weights = lax.dynamic_slice_in_dim(obs_weight, mem_index * own, own, 0)
    count = lax.dynamic_slice_in_dim(counts, mem_index, 1, 0)[0]
    region_state, region_obs = (
        lax.all_to_all(state, "mem", split_axis=1, concat_axis=0, tiled=True),
        lax.all_to_all(obs_ens, "mem", split_axis=1, concat_axis=0, tiled=True),
    )
    members = region_obs.shape[0]
    full_obs = region_obs.astype(jnp.float32)
    obs_centre = jnp.mean(full_obs, axis=0)
    mask = (jnp.arange(own, dtype=jnp.int32) < count).astype(jnp.float32)
    root = jnp.sqrt(weights * mask)
    own_gains = ((full_obs - obs_centre[None, :]) * root[None, :]).astype(jnp.bfloat16)
    own_innov = (root * (values - obs_centre)).astype(jnp.bfloat16)
    stacked = jnp.concatenate([own_gains, own_innov[None, :]], axis=0)
    inner = cross_product(own_gains, own_gains)
    widened = extended(stacked, (("patch", 1),), half)
    gains = widened[:-1]
    innov = widened[-1].astype(jnp.float32)
    edges = jnp.concatenate([gains[:, :half], gains[:, half + own :]], axis=1)
    crossed = cross_product(edges, own_gains)
    corner = cross_product(edges, edges)
    top = jnp.concatenate([corner[:half, :half], crossed[:half], corner[:half, half:]], axis=1)
    middle = jnp.concatenate([crossed[:half].T, inner, crossed[half:].T], axis=1)
    bottom = jnp.concatenate([corner[half:, :half], crossed[half:], corner[half:, half:]], axis=1)
    normal = jnp.concatenate([top, middle, bottom], axis=0) / (members - 1)
    upper = jnp.max(jnp.sum(jnp.abs(normal), axis=1)) + 1e-06
    shifted = normal * (2.0 / upper) - jnp.eye(normal.shape[0], dtype=jnp.float32)
    full = region_state.astype(jnp.float32)
    centre = jnp.mean(full, axis=0)
    spread = (full - centre[None, :]).astype(jnp.bfloat16)
    product = cross_product(spread, gains)
    mixed = clenshaw(product, shifted, chebyshev(upper, root_curve)).astype(jnp.bfloat16)
    mean_weights = clenshaw(innov[None, :], shifted, chebyshev(upper, inverse_curve))[0]
    mean_shift = jnp.dot(product, mean_weights, precision=lax.Precision.HIGHEST) / (members - 1)
    update = lax.dot_general(
        gains, mixed, (((1,), (1,)), ((), ())), preferred_element_type=jnp.float32
    ) / (members - 1)
    analysed = (full + mean_shift[None, :] + update).astype(jnp.bfloat16)
    return lax.all_to_all(analysed, "mem", split_axis=0, concat_axis=1, tiled=True)


def solution(mesh):
    placed = (P("mem", "patch"), P("mem", "patch"), P("patch"), P("patch"), P("patch"))
    return jax.shard_map(
        on_device, mesh=mesh, in_specs=placed, out_specs=P("mem", "patch"), check_vma=False
    )
```

profile of v0, /device:TPU:2, one launch (start us, length us, event | category | flops | bytes accessed | tf_op | source)
XLA Modules:
  0.0 127.7 jit_solution(8826710096986276952)
XLA Ops:
  0.0 2.0 %copy.22 = bf16[4,32,8,256]{3,2,0,1:T(8,128)(2,1)} copy(bf16[4,32,8,256]{3,2,1,0:T(8,128)(2,1)} %bitcast.114) | data formatting | bytes 1048576 | tf_op jit(solution)/shard_map/all_to_all | solution.py:75
  2.0 13.1 %all-to-all-start.1 = ((bf16[32,32,256]{2,0,1:T(8,128)(2,1)}), bf16[32,32,256]{2,0,1:T(8,128)(2,1)S(1)}, u32[]{:S(2)}, u32[]{:S(2)}) async-start(bf16[32,32,256]{2,0,1:T(8,128)(2,1)} %bitcast.110), calls=%async_computation.1 | async-start | bytes 1048576 | tf_op jit(solution)/shard_map/all_to_all | solution.py:75
  15.1 1.1 copy.21
  16.8 12.2 %all-to-all-done.1 = bf16[32,32,256]{2,0,1:T(8,128)(2,1)S(1)} async-done(((bf16[32,32,256]{2,0,1:T(8,128)(2,1)}), bf16[32,32,256]{2,0,1:T(8,128)(2,1)S(1)}, u32[]{:S(2)}, u32[]{:S(2)}) %all-to-all-start.1) | async-done | bytes 524320 | tf_op jit(solution)/shard_map/all_to_all | solution.py:75
  29.1 5.6 %all-to-all-start = ((bf16[32,32,512]{2,0,1:T(8,128)(2,1)}), bf16[32,32,512]{2,0,1:T(8,128)(2,1)S(1)}, u32[]{:S(2)}, u32[]{:S(2)}) async-start(bf16[32,32,512]{2,0,1:T(8,128)(2,1)} %bitcast.109), calls=%async_computation | async-start | bytes 2097152 | tf_op jit(solution)/shard_map/all_to_all | solution.py:74
  34.8 1.4 %multiply_convert_fusion.1 = (bf16[256]{0:T(256)(128)(2,1)S(1)}, f32[256]{0:T(256)S(1)}, f32[256]{0:T(256)S(1)}) fusion(f32[8192]{0:T(1024)} %param.7, s32[]{:T(128)S(6)} %select_n.15, f32[256]{0:T(256)S(1)} %convert_reduce_fusion.1, f32[8192]{0:T(1024)} %param.8, s32[]{:T(128)} %bitcast.5), kind=kLoop, calls=%fused_computation.80 | loop fusion | flops 1536 | bytes 5640 | tf_op jit(solution)/shard_map/convert_element_type | solution.py:83
  36.5 10.7 %collective-permute-start.1 = (bf16[1025,128]{1,0:T(8,128)(2,1)S(1)}, bf16[1025,128]{1,0:T(8,128)(2,1)S(1)}, u32[]{:S(2)}, u32[]{:S(2)}) collective-permute-start(bf16[1025,128]{1,0:T(8,128)(2,1)S(1)} %get-tuple-element.12), channel_id=1, source_target_pairs={{1,0},{2,1},{3,2},{4,3},{5,4},{6,5},{7,6},{8,7},{9,8},{10,9},{11,1... | collective-permute-start | bytes 787208 | tf_op jit(solution)/shard_map/ppermute | solution.py:20
  47.5 3.6 %collective-permute-done = bf16[1025,128]{1,0:T(8,128)(2,1)S(1)} collective-permute-done((bf16[1025,128]{1,0:T(8,128)(2,1)S(1)}, bf16[1025,128]{1,0:T(8,128)(2,1)S(1)}, u32[]{:S(2)}, u32[]{:S(2)}) %collective-permute-start) | collective-permute-done | bytes 262432 | tf_op jit(solution)/shard_map/ppermute | solution.py:18
  54.6 1.2 convert_subtract_fusion
  57.4 4.3 %broadcast_multiply_fusion.8 = (f32[1,512]{1,0:T(1,128)S(1)}, f32[1,512]{1,0:T(1,128)S(1)}, f32[1,512]{1,0:T(1,128)S(1)}, f32[1,512]{1,0:T(1,128)S(1)}, f32[1,51...) fusion(f32[1,512]{1,0:T(1,128)S(1)} %get-tuple-element.8, f32[]{:T(128)} %bitcast.10, f32[]{:T(128)} %bitcast.22, ...), kind=kLoop, calls=%fused_computation.79 | loop fusion | flops 3584 | bytes 16412 | tf_op jit(solution)/shard_map/mul | solution.py:57
  62.7 1.0 fusion.39
  69.3 1.1 pad_maximum_fusion
  70.9 1.0 copy-done
  72.6 1.0 fusion.45
  73.6 3.1 %multiply_add_fusion = f32[512,512]{1,0:T(8,128)S(1)} fusion(f32[512,512]{1,0:T(8,128)S(1)} %fusion.13, f32[512,512]{0,1:T(8,128)S(1)} %convert_subtract_fusion, f32[]{:T(128)} %bitcast.49, f32[]{:T(128)} %bitcast.48), kind=kOutput, calls=%fused_computation.27 | convolution fusion | flops 1611661312 | bytes 3145736 | tf_op jit(solution)/shard_map/dot_general | solution.py:53
  76.7 2.1 %convolution_multiply_fusion.4 = f32[512,512]{1,0:T(8,128)S(1)} fusion(f32[512,512]{1,0:T(8,128)S(1)} %multiply_add_fusion, f32[512,512]{0,1:T(8,128)S(1)} %convert_subtract_fusion), kind=kOutput, calls=%fused_computation.10 | convolution fusion | flops 1610874880 | bytes 3145728 | tf_op jit(solution)/shard_map/dot_general | solution.py:53
  78.8 3.9 %add_subtract_fusion.2 = f32[512,512]{1,0:T(8,128)S(1)} fusion(f32[512,512]{1,0:T(8,128)S(1)} %multiply_add_fusion, f32[512,512]{1,0:T(8,128)S(1)} %fusion.13, f32[512,512]{0,1:T(8,128)S(1)} %convert_subtract_fusion, f32[512,512]{1,0:T(8,128)S(1)} %convolution_multiply_fusion.4, f32[]{:T(128)} %bitcast.49, f32[]{:T(128)} %bitcast.47, f32[]{:T(128)} %bitcast.46), kind=kOutput, calls=%fused_computation.25 | convolution fusion | flops 1612709888 | bytes 5242892 | tf_op jit(solution)/shard_map/dot_general | solution.py:53
  82.7 3.8 %add_subtract_fusion.1 = f32[512,512]{1,0:T(8,128)S(1)} fusion(f32[512,512]{1,0:T(8,128)S(1)} %fusion.13, f32[512,512]{1,0:T(8,128)S(1)} %convolution_multiply_fusion.4, f32[512,512]{1,0:T(8,128)S(1)} %add_subtract_fusion.2, f32[512,512]{0,1:T(8,128)S(1)} %convert_subtract_fusion, f32[]{:T(128)} %bitcast.49, f32[]{:T(128)} %bitcast.47, f32[]{:T(128)} %bitcast.45), kind=kOutput, calls=%fused_computation.24 | convolution fusion | flops 1612709888 | bytes 5242892 | tf_op jit(solution)/shard_map/dot_general | solution.py:53
  86.5 2.5 %add_subtract_fusion = f32[512,512]{1,0:T(8,128)S(1)} fusion(f32[512,512]{1,0:T(8,128)S(1)} %add_subtract_fusion.2, f32[512,512]{1,0:T(8,128)S(1)} %fusion.13, f32[512,512]{1,0:T(8,128)S(1)} %add_subtract_fusion.1, f32[512,512]{0,1:T(8,128)S(1)} %convert_subtract_fusion, f32[]{:T(128)} %bitcast.44), kind=kOutput, calls=%fused_computation.23 | convolution fusion | flops 1611661312 | bytes 5242884 | tf_op jit(solution)/shard_map/dot_general | solution.py:53
  89.0 1.9 %convolution_multiply_fusion = f32[512,512]{1,0:T(8,128)S(1)} fusion(f32[512,512]{1,0:T(8,128)S(1)} %add_subtract_fusion, f32[512,512]{0,1:T(8,128)S(1)} %convert_subtract_fusion), kind=kOutput, calls=%fused_computation.6 | convolution fusion | flops 1610874880 | bytes 3145728 | tf_op jit(solution)/shard_map/dot_general | solution.py:53
  90.9 2.7 %fusion.5 = f32[512,512]{1,0:T(8,128)S(1)} fusion(f32[512,512]{0,1:T(8,128)S(1)} %convert_subtract_fusion, f32[512,512]{1,0:T(8,128)S(1)} %add_subtract_fusion.1, f32[512,512]{1,0:T(8,128)S(1)} %convolution_multiply_fusion, f32[512,512]{1,0:T(8,128)S(1)} %fusion.13, f32[]{:T(128)} %bitcast.43), kind=kOutput, calls=%fused_computation.20 | convolution fusion | flops 1611399168 | bytes 5242884 | tf_op jit(solution)/shard_map/dot_general | solution.py:57
  93.5 1.4 %fusion.2 = bf16[1024,512]{1,0:T(8,128)(2,1)S(1)} fusion(bf16[32,32,512]{2,0,1:T(8,128)(2,1)S(1)} %all-to-all-done, f32[512]{0:T(512)S(1)} %broadcast_multiply_fusion, bf16[1025,512]{1,0:T(8,128)(2,1)S(1)} %copy-done, f32[512,512]{1,0:T(8,128)S(1)} %add_subtract_fusion, f32[512,512]{1,0:T(8,128)S(1)} %fusion.5, f32[512,512]{1,0:T(8,128)S(1)} %fusion.13, ...), kind=kOutput, calls=%fused_computation.5 | convolution fusion | flops 540540928 | bytes 6293508 | tf_op jit(solution)/shard_map/dot_general | solution.py:105
  95.0 31.6 %all_to_all.45 = bf16[32,32,512]{2,1,0:T(8,128)(2,1)S(1)} all-to-all(bf16[32,32,512]{2,1,0:T(8,128)(2,1)S(1)} %bitcast.112), channel_id=1, replica_groups=mesh['mem'=32,'patch'=24] {'mem'}, dimensions={0} | all-to-all | bytes 2097152 | tf_op jit(solution)/shard_map/all_to_all | solution.py:109
  126.6 1.1 copy.18
  (66 shorter events, 13.2 us)
Async XLA Ops:
  0.0 15.1 %copy-start.2 = (bf16[32,16384]{1,0:T(8,128)(2,1)S(1)}, bf16[32,16384]{1,0:T(8,128)(2,1)}, u32[]{:S(2)}) copy-start(bf16[32,16384]{1,0:T(8,128)(2,1)} %param.5) | copy-start | bytes 3145732
  2.0 27.1 %all-to-all-start.1 = ((bf16[32,32,256]{2,0,1:T(8,128)(2,1)}), bf16[32,32,256]{2,0,1:T(8,128)(2,1)S(1)}, u32[]{:S(2)}, u32[]{:S(2)}) async-start(bf16[32,32,256]{2,0,1:T(8,128)(2,1)} %bitcast.110), calls=%async_computation.1 | async-start | bytes 1048576 | tf_op jit(solution)/shard_map/all_to_all | solution.py:75
  15.1 1.1 copy-start.10
  29.1 41.4 %all-to-all-start = ((bf16[32,32,512]{2,0,1:T(8,128)(2,1)}), bf16[32,32,512]{2,0,1:T(8,128)(2,1)S(1)}, u32[]{:S(2)}, u32[]{:S(2)}) async-start(bf16[32,32,512]{2,0,1:T(8,128)(2,1)} %bitcast.109), calls=%async_computation | async-start | bytes 2097152 | tf_op jit(solution)/shard_map/all_to_all | solution.py:74
  36.4 14.7 %collective-permute-start = (bf16[1025,128]{1,0:T(8,128)(2,1)S(1)}, bf16[1025,128]{1,0:T(8,128)(2,1)S(1)}, u32[]{:S(2)}, u32[]{:S(2)}) collective-permute-start(bf16[1025,128]{1,0:T(8,128)(2,1)S(1)} %get-tuple-element.11), channel_id=1, source_target_pairs={{0,1},{1,2},{2,3},{3,4},{4,5},{5,6},{6,7},{7,8},{8,9},{9,10},{10,1... | collective-permute-start | bytes 787208 | tf_op jit(solution)/shard_map/ppermute | solution.py:18
  36.5 14.7 %collective-permute-start.1 = (bf16[1025,128]{1,0:T(8,128)(2,1)S(1)}, bf16[1025,128]{1,0:T(8,128)(2,1)S(1)}, u32[]{:S(2)}, u32[]{:S(2)}) collective-permute-start(bf16[1025,128]{1,0:T(8,128)(2,1)S(1)} %get-tuple-element.12), channel_id=1, source_target_pairs={{1,0},{2,1},{3,2},{4,3},{5,4},{6,5},{7,6},{8,7},{9,8},{10,9},{11,1... | collective-permute-start | bytes 787208 | tf_op jit(solution)/shard_map/ppermute | solution.py:20
  47.5 4.8 %copy-start.3 = (f32[256,256]{0,1:T(8,128)}, f32[256,256]{0,1:T(8,128)S(1)}, u32[]{:S(2)}) copy-start(f32[256,256]{0,1:T(8,128)S(1)} %convolution_bitcast_fusion) | copy-start | bytes 786436
  52.0 0.6 copy-start.4
  52.0 0.6 copy-start.5
  52.0 0.7 copy-start.6
  52.0 0.7 copy-start.7
  52.1 2.6 %copy-start.1 = (f32[128,256]{0,1:T(8,128)}, f32[128,256]{0,1:T(8,128)S(1)}, u32[]{:S(2)}) copy-start(f32[128,256]{0,1:T(8,128)S(1)} %get-tuple-element.20) | copy-start | bytes 393220
  54.6 1.3 copy-start.8
  54.6 1.3 copy-start.9
  70.6 1.2 copy-start
where the time goes:
time: 128 us
  blocking collectives  31.6 us (25%)
  matrix products  30.9 us (24%)
  starting transfers between devices  29.3 us (23%)
  waiting for transfers between devices  15.9 us (12%)
  other arithmetic  11.2 us (9%)
  local copies, waits for them, and re-layouts  7.69 us (6%)
    all_to_all x1, blocking collectives, on_device(): lax.all_to_all(analysed, 'mem', split_axis=0, concat_axis=1, tiled=True)  31.6 us
    dot_general x14, matrix products, clenshaw(): jnp.dot(nearer, matrix, precision=lax.Precision.HIGHEST)  26.7 us
    all_to_all x1, starting transfers between devices, on_device(): lax.all_to_all(obs_ens, 'mem', split_axis=1, concat_axis=0, tiled=True)  13.1 us
    all_to_all x1, waiting for transfers between devices, on_device(): lax.all_to_all(obs_ens, 'mem', split_axis=1, concat_axis=0, tiled=True)  12.2 us
    ppermute x1, starting transfers between devices, extended(): lax.ppermute(head, axis, [((i + 1) % count, i) for i in range(count)])  10.7 us
    all_to_all x1, starting transfers between devices, on_device(): lax.all_to_all(state, 'mem', split_axis=1, concat_axis=0, tiled=True)  5.56 us
    mul x1, other arithmetic, clenshaw(): coefs[0] * block + jnp.dot(nearer, matrix, precision=lax.Precision.HIGHEST)  4.33 us
    ppermute x1, waiting for transfers between devices, extended(): lax.ppermute(tail, axis, [(i, (i + 1) % count) for i in range(count)])  3.64 us
  transfers between devices with their start and end apart: 4, of which 2 were waited for; matrix products, arithmetic and copies ran while one was open for 17% of the time, Pallas kernels for 0%

commit v1 on v0

v1 whole, which is shorter than its diff:
```python
import math

import jax
import jax.numpy as jnp
import numpy as np
from jax import lax
from jax.experimental import pallas as pl
from jax.experimental.pallas import tpu as pltpu
from jax.sharding import PartitionSpec as P

DEGREE = 7
NODES = DEGREE + 1
PAD = 16
LIMIT = 30 * 1024 * 1024


def tables():
    theta = (np.arange(NODES) + 0.5) * (math.pi / NODES)
    orders = np.arange(NODES)
    table = np.zeros((2 * NODES, 128), np.float32)
    weight = np.where(orders == 0, 0.5, 1.0) * 2.0 / NODES
    table[:NODES, :NODES] = np.cos(orders[:, None] * theta[None, :]) * weight[:, None]
    table[NODES, :NODES] = (np.cos(theta) + 1.0) * 0.5
    return table


def dot(left, right):
    return jnp.dot(left, right, preferred_element_type=jnp.float32)


def split(x):
    high = x.astype(jnp.bfloat16)
    return high, (x - high.astype(jnp.float32)).astype(jnp.bfloat16)


def product(left, right):
    return dot(left[0], right[0]) + (dot(left[0], right[1]) + dot(left[1], right[0]))


def gains_kernel(obs_ref, side_ref, head_ref, tail_ref):
    members, own = obs_ref.shape
    half = own // 2
    for part, out in ((0, head_ref), (1, tail_ref)):
        columns = slice(part * half, (part + 1) * half)
        full = obs_ref[:, columns].astype(jnp.float32)
        centre = jnp.sum(full, axis=0, keepdims=True) * (1.0 / members)
        root = side_ref[0:1, columns]
        out[0:members, :] = ((full - centre) * root).astype(jnp.bfloat16)
        innov = root * (side_ref[1:2, columns] - centre)
        out[members:, :] = jnp.broadcast_to(innov, (PAD, half)).astype(jnp.bfloat16)


def weights_kernel(left_ref, head_ref, tail_ref, right_ref, table_ref, out_ref, gains, turned):
    members, sites = gains.shape
    half = sites // 4
    parts = (left_ref, head_ref, tail_ref, right_ref)
    for part, ref in enumerate(parts):
        block = ref[0:members, :]
        gains[:, part * half : (part + 1) * half] = block
        turned[part * half : (part + 1) * half, :] = block.T
    innov = jnp.concatenate([ref[members:, :] for ref in parts], axis=1)

    normal = dot(turned[...], gains[...]) * (1.0 / (members - 1))
    upper = jnp.max(jnp.sum(jnp.abs(normal), axis=0, keepdims=True), axis=1, keepdims=True) + 1e-06
    nodes = upper * table_ref[NODES : NODES + 1, :]
    lifted = jnp.sqrt(1.0 + nodes)
    table = table_ref[0:NODES, :]
    roots = jnp.sum(table * (-1.0 / (lifted * (1.0 + lifted))), axis=1, keepdims=True)
    inverses = jnp.sum(table * (1.0 / (1.0 + nodes)), axis=1, keepdims=True)
    a = [roots[k : k + 1, :] for k in range(NODES)]
    e = [inverses[k : k + 1, :] for k in range(NODES)]

    rows = lax.broadcasted_iota(jnp.int32, normal.shape, 0)
    columns = lax.broadcasted_iota(jnp.int32, normal.shape, 1)
    eye = jnp.where(rows == columns, 1.0, 0.0).astype(jnp.float32)
    scaled = normal * (2.0 / upper)
    scaled_parts = split(scaled)
    t1 = scaled - eye
    t2 = 2.0 * product(scaled_parts, scaled_parts) - 4.0 * scaled + eye
    t2_parts = split(t2)
    t3 = 2.0 * (product(t2_parts, scaled_parts) - t2) - t1
    t4 = 2.0 * product(t2_parts, t2_parts) - eye
    t4_parts = split(t4)

    def polynomial(c):
        inner = c[5] * t1 + c[6] * t2 + c[7] * t3
        outer = c[0] * eye + (c[1] - c[7]) * t1 + (c[2] - c[6]) * t2 + (c[3] - c[5]) * t3 + c[4] * t4
        return outer + 2.0 * product(split(inner), t4_parts)

    root = split(polynomial(a))
    inverse = split(polynomial(e))
    mean_weights = dot(innov, inverse[0]) + dot(innov, inverse[1])
    shift = split(mean_weights * (1.0 / (members - 1)))
    turned_now = turned[...]
    rows_shift = dot(shift[0], turned_now) + dot(shift[1], turned_now)
    high, low = split(rows_shift)
    out_ref[members:, :] = jnp.concatenate([high[: PAD // 2], low[: PAD // 2]], axis=0)
    reduced = (dot(root[0], turned_now) + dot(root[1], turned_now)).astype(jnp.bfloat16)
    out_ref[0:members, :] = (dot(gains[...], reduced) * (1.0 / (members - 1))).astype(jnp.bfloat16)


def apply_kernel(state_ref, weights_ref, out_ref, spread):
    members = state_ref.shape[0]
    total = jnp.sum(state_ref[...].astype(jnp.float32), axis=0, keepdims=True)
    centre = total * (1.0 / members)
    spread[...] = (state_ref[...].astype(jnp.float32) - centre).astype(jnp.bfloat16)
    shifts = dot(weights_ref[members:, :], spread[...])
    shift = shifts[0:1, :] + shifts[PAD // 2 : PAD // 2 + 1, :]
    step = 256
    for start in range(0, members, step):
        block = slice(start, start + step)
        update = dot(weights_ref[block, :], spread[...])
        out_ref[block, :] = (state_ref[block, :].astype(jnp.float32) + shift + update).astype(jnp.bfloat16)


def call(kernel, out_shape, scratch, flops, nbytes, *args):
    return pl.pallas_call(
        kernel,
        out_shape=out_shape,
        in_specs=[pl.BlockSpec(memory_space=pltpu.VMEM)] * len(args),
        out_specs=jax.tree.map(lambda _: pl.BlockSpec(memory_space=pltpu.VMEM), out_shape),
        scratch_shapes=scratch,
        compiler_params=pltpu.CompilerParams(vmem_limit_bytes=LIMIT),
        cost_estimate=pl.CostEstimate(flops=flops, bytes_accessed=nbytes, transcendentals=0),
    )(*args)


def on_device(state, obs_ens, obs_values, obs_weight, counts):
    mem_index = lax.axis_index("mem")
    own = obs_ens.shape[1] // lax.axis_size("mem")
    half = own // 2
    patches = lax.axis_size("patch")
    region_obs = lax.all_to_all(obs_ens, "mem", split_axis=1, concat_axis=0, tiled=True)
    region_state = lax.all_to_all(state, "mem", split_axis=1, concat_axis=0, tiled=True)
    members, columns = region_state.shape

    values = lax.dynamic_slice_in_dim(obs_values, mem_index * own, own, 0)
    weights = lax.dynamic_slice_in_dim(obs_weight, mem_index * own, own, 0)
    count = lax.dynamic_slice_in_dim(counts, mem_index, 1, 0)[0]
    mask = (jnp.arange(own, dtype=jnp.int32) < count).astype(jnp.float32)
    side = jnp.stack([jnp.sqrt(weights * mask), values])

    edge = jax.ShapeDtypeStruct((members + PAD, half), jnp.bfloat16)
    head, tail = call(gains_kernel, (edge, edge), [], 10**6, 2 * 10**6, region_obs, side)
    left = lax.ppermute(tail, "patch", [(i, (i + 1) % patches) for i in range(patches)])
    right = lax.ppermute(head, "patch", [((i + 1) % patches, i) for i in range(patches)])
    sites = 2 * own
    transform = call(
        weights_kernel,
        jax.ShapeDtypeStruct((members + PAD, members), jnp.bfloat16),
        [pltpu.VMEM((members, sites), jnp.bfloat16), pltpu.VMEM((sites, members), jnp.bfloat16)],
        7 * 10**9, 4 * 10**6,
        left, head, tail, right, jnp.asarray(tables()),
    )
    analysed = call(
        apply_kernel,
        jax.ShapeDtypeStruct((members, columns), jnp.bfloat16),
        [pltpu.VMEM((members, columns), jnp.bfloat16)],
        2 * 10**9, 4 * 10**6,
        region_state, transform,
    )
    return lax.all_to_all(analysed, "mem", split_axis=0, concat_axis=1, tiled=True)


def solution(mesh):
    placed = (P("mem", "patch"), P("mem", "patch"), P("patch"), P("patch"), P("patch"))
    return jax.shard_map(
        on_device, mesh=mesh, in_specs=placed, out_specs=P("mem", "patch"), check_vma=False
    )
```

time: 128 us -> 101 us (0.79)
  the two profiles are of different devices: /device:TPU:2 before, /device:TPU:209 now
where the time goes in v1:
time: 101 us
  blocking collectives  37.7 us (37%)
  waiting for transfers between devices  21.5 us (21%)
  starting transfers between devices  21.1 us (21%)
  Pallas kernels  10.5 us (10%)
  local copies, waits for them, and re-layouts  8.51 us (8%)
  other arithmetic  1.4 us (1%)
    all_to_all x1, blocking collectives, on_device(): lax.all_to_all(analysed, 'mem', split_axis=0, concat_axis=1, tiled=True)  37.7 us
    all_to_all x1, waiting for transfers between devices, on_device(): lax.all_to_all(obs_ens, 'mem', split_axis=1, concat_axis=0, tiled=True)  14.1 us
    pallas_call x3, Pallas kernels, call(): pl.pallas_call(kernel, out_shape=out_shape, in_specs=[pl.BlockSpec(memory...  10.5 us
    all_to_all x1, starting transfers between devices, on_device(): lax.all_to_all(obs_ens, 'mem', split_axis=1, concat_axis=0, tiled=True)  9.49 us
    all_to_all x1, starting transfers between devices, on_device(): lax.all_to_all(state, 'mem', split_axis=1, concat_axis=0, tiled=True)  6.22 us
    ppermute x1, starting transfers between devices, on_device(): lax.ppermute(tail, 'patch', [(i, (i + 1) % patches) for i in range(patche...  5.35 us
    ppermute x1, waiting for transfers between devices, on_device(): lax.ppermute(head, 'patch', [((i + 1) % patches, i) for i in range(patche...  3.99 us
    ppermute x1, waiting for transfers between devices, on_device(): lax.ppermute(tail, 'patch', [(i, (i + 1) % patches) for i in range(patche...  3.36 us
  transfers between devices with their start and end apart: 4, of which 3 were waited for; matrix products, arithmetic and copies ran while one was open for 4% of the time, Pallas kernels for 9%

profile of v1, /device:TPU:209, one launch (start us, length us, event | category | flops | bytes accessed | tf_op | source)
XLA Modules:
  0.0 100.7 jit_solution(14946438583594266171)
XLA Ops:
  0.0 2.0 %copy.16 = bf16[4,32,8,256]{3,2,0,1:T(8,128)(2,1)} copy(bf16[4,32,8,256]{3,2,1,0:T(8,128)(2,1)} %bitcast.26) | data formatting | bytes 1048576 | tf_op jit(solution)/shard_map/all_to_all | solution.py:133
  2.0 9.5 %all-to-all-start.1 = ((bf16[32,32,256]{2,0,1:T(8,128)(2,1)}), bf16[32,32,256]{2,0,1:T(8,128)(2,1)S(1)}, u32[]{:S(2)}, u32[]{:S(2)}) async-start(bf16[32,32,256]{2,0,1:T(8,128)(2,1)} %bitcast.20), calls=%async_computation.1 | async-start | bytes 1048576 | tf_op jit(solution)/shard_map/all_to_all | solution.py:133
  11.5 0.0 copy-start.4
  11.5 0.0 copy-done.3
  11.5 0.0 copy-start
  11.5 1.1 %copy.15 = bf16[4,32,8,512]{3,2,0,1:T(8,128)(2,1)} copy(bf16[4,32,8,512]{3,2,1,0:T(8,128)(2,1)S(1)} %bitcast.25) | data formatting | bytes 2097152 | tf_op jit(solution)/shard_map/all_to_all | solution.py:134
  12.6 14.1 %all-to-all-done.1 = bf16[32,32,256]{2,0,1:T(8,128)(2,1)S(1)} async-done(((bf16[32,32,256]{2,0,1:T(8,128)(2,1)}), bf16[32,32,256]{2,0,1:T(8,128)(2,1)S(1)}, u32[]{:S(2)}, u32[]{:S(2)}) %all-to-all-start.1) | async-done | bytes 524320 | tf_op jit(solution)/shard_map/all_to_all | solution.py:133
  26.7 6.2 %all-to-all-start = ((bf16[32,32,512]{2,0,1:T(8,128)(2,1)}), bf16[32,32,512]{2,0,1:T(8,128)(2,1)S(1)}, u32[]{:S(2)}, u32[]{:S(2)}) async-start(bf16[32,32,512]{2,0,1:T(8,128)(2,1)} %bitcast.19), calls=%async_computation | async-start | bytes 2097152 | tf_op jit(solution)/shard_map/all_to_all | solution.py:134
  33.0 0.0 copy-done.4
  33.0 0.7 dynamic_slice.9
  33.6 0.8 dynamic_slice.11
  34.4 1.4 %fusion = f32[256]{0:T(256)S(1)} fusion(f32[8192]{0:T(1024)} %param.9, s32[]{:T(128)S(6)} %select_n.8, s32[]{:T(128)} %bitcast.4), kind=kLoop, calls=%fused_computation.4 | loop fusion | flops 512 | bytes 2056 | tf_op jit(solution)/shard_map/sqrt | solution.py:141
  35.8 0.3 shard_map.64
  36.1 5.4 %collective-permute-start = (bf16[1040,128]{1,0:T(8,128)(2,1)S(1)}, bf16[1040,128]{1,0:T(8,128)(2,1)S(1)}, u32[]{:S(2)}, u32[]{:S(2)}) collective-permute-start(bf16[1040,128]{1,0:T(8,128)(2,1)S(1)} %get-tuple-element.7.tail_ref), channel_id=1, source_target_pairs={{0,1},{1,2},{2,3},{3,4},{4,5},{5,6},{6,7},{7,8},{8,9},{9,10},{10,1... | collective-permute-start | bytes 798728 | tf_op jit(solution)/shard_map/ppermute | solution.py:145
  41.4 0.0 collective-permute-start.1
  41.4 3.4 %collective-permute-done.left_ref = bf16[1040,128]{1,0:T(8,128)(2,1)S(1)} collective-permute-done((bf16[1040,128]{1,0:T(8,128)(2,1)S(1)}, bf16[1040,128]{1,0:T(8,128)(2,1)S(1)}, u32[]{:S(2)}, u32[]{:S(2)}) %collective-permute-start) | collective-permute-done | bytes 266272 | tf_op jit(solution)/shard_map/ppermute | solution.py:145
  44.8 4.0 %collective-permute-done.1.right_ref = bf16[1040,128]{1,0:T(8,128)(2,1)S(1)} collective-permute-done((bf16[1040,128]{1,0:T(8,128)(2,1)S(1)}, bf16[1040,128]{1,0:T(8,128)(2,1)S(1)}, u32[]{:S(2)}, u32[]{:S(2)}) %collective-permute-start.1) | collective-permute-done | bytes 266272 | tf_op jit(solution)/shard_map/ppermute | solution.py:146
  48.8 8.6 %shard_map.65.weights_ref = bf16[1040,1024]{1,0:T(8,128)(2,1)S(1)} custom-call(bf16[1040,128]{1,0:T(8,128)(2,1)S(1)} %collective-permute-done.left_ref, bf16[1040,128]{1,0:T(8,128)(2,1)S(1)} %get-tuple-element.8.head_ref, bf16[1040,128]{1,0:T(8,128)(2,1)S(1)} %get-tuple-element.7.tail_ref, bf16[1040,128]{1,0:T(8,128)(2,1)S(1)} %collective-permute-done.1.right_ref, ...), custom_call_target="tpu_custom_call" | custom-call | flops 7000000000 | bytes 4000000 | tf_op jit(solution)/shard_map/pallas_call | solution.py:117
  57.4 1.3 %copy-done.1 = bf16[1040,1024]{1,0:T(8,128)(2,1)} copy-done((bf16[1040,1024]{1,0:T(8,128)(2,1)}, bf16[1040,1024]{1,0:T(8,128)(2,1)S(1)}, u32[]{:S(2)}) %copy-start.1) | copy-done | bytes 2129944
  58.7 0.0 all-to-all-done
  58.7 1.6 %copy-done.2 = bf16[1040,1024]{1,0:T(8,128)(2,1)S(1)} copy-done((bf16[1040,1024]{1,0:T(8,128)(2,1)S(1)}, bf16[1040,1024]{1,0:T(8,128)(2,1)}, u32[]{:S(2)}) %copy-start.2) | copy-done | bytes 2129944
  60.3 1.7 %shard_map.66 = bf16[1024,512]{1,0:T(8,128)(2,1)S(1)} custom-call(bf16[1024,512]{1,0:T(8,128)(2,1)S(1)} %bitcast.22, bf16[1040,1024]{1,0:T(8,128)(2,1)S(1)} %copy-done.2), custom_call_target="tpu_custom_call" | custom-call | flops 2000000000 | bytes 4000000 | tf_op jit(solution)/shard_map/pallas_call | solution.py:117
  62.0 37.7 %all_to_all.57 = bf16[32,32,512]{2,1,0:T(8,128)(2,1)S(1)} all-to-all(bf16[32,32,512]{2,1,0:T(8,128)(2,1)S(1)} %bitcast.23), channel_id=1, replica_groups=mesh['mem'=32,'patch'=24] {'mem'}, dimensions={0} | all-to-all | bytes 2097152 | tf_op jit(solution)/shard_map/all_to_all | solution.py:162
  99.7 1.1 %copy.12 = bf16[32,4,8,512]{3,2,0,1:T(8,128)(2,1)} copy(bf16[32,4,8,512]{3,2,1,0:T(8,128)(2,1)S(1)} %bitcast.24) | data formatting | bytes 2097152 | tf_op jit(solution)/shard_map/all_to_all | solution.py:162
  (5 shorter events, 0.0 us)
Async XLA Ops:
  0.0 11.5 %copy-start.3 = (bf16[32,16384]{1,0:T(8,128)(2,1)S(1)}, bf16[32,16384]{1,0:T(8,128)(2,1)}, u32[]{:S(2)}) copy-start(bf16[32,16384]{1,0:T(8,128)(2,1)} %param.6) | copy-start | bytes 3145732
  2.0 24.8 %all-to-all-start.1 = ((bf16[32,32,256]{2,0,1:T(8,128)(2,1)}), bf16[32,32,256]{2,0,1:T(8,128)(2,1)S(1)}, u32[]{:S(2)}, u32[]{:S(2)}) async-start(bf16[32,32,256]{2,0,1:T(8,128)(2,1)} %bitcast.20), calls=%async_computation.1 | async-start | bytes 1048576 | tf_op jit(solution)/shard_map/all_to_all | solution.py:133
  11.5 21.5 %copy-start.4 = (s32[32]{0:T(128)S(1)}, s32[32]{0:T(128)}, u32[]{:S(2)}) copy-start(s32[32]{0:T(128)} %param.10) | copy-start | bytes 388
  11.5 37.3 %copy-start = (f32[16,128]{1,0:T(8,128)S(1)}, f32[16,128]{1,0:T(8,128)}, u32[]{:S(2)}) copy-start(f32[16,128]{1,0:T(8,128)} %constant.17.clone.table_ref) | copy-start | bytes 24580
  26.7 32.0 %all-to-all-start = ((bf16[32,32,512]{2,0,1:T(8,128)(2,1)}), bf16[32,32,512]{2,0,1:T(8,128)(2,1)S(1)}, u32[]{:S(2)}, u32[]{:S(2)}) async-start(bf16[32,32,512]{2,0,1:T(8,128)(2,1)} %bitcast.19), calls=%async_computation | async-start | bytes 2097152 | tf_op jit(solution)/shard_map/all_to_all | solution.py:134
  36.1 8.7 %collective-permute-start = (bf16[1040,128]{1,0:T(8,128)(2,1)S(1)}, bf16[1040,128]{1,0:T(8,128)(2,1)S(1)}, u32[]{:S(2)}, u32[]{:S(2)}) collective-permute-start(bf16[1040,128]{1,0:T(8,128)(2,1)S(1)} %get-tuple-element.7.tail_ref), channel_id=1, source_target_pairs={{0,1},{1,2},{2,3},{3,4},{4,5},{5,6},{6,7},{7,8},{8,9},{9,10},{10,1... | collective-permute-start | bytes 798728 | tf_op jit(solution)/shard_map/ppermute | solution.py:145
  41.4 7.3 %collective-permute-start.1 = (bf16[1040,128]{1,0:T(8,128)(2,1)S(1)}, bf16[1040,128]{1,0:T(8,128)(2,1)S(1)}, u32[]{:S(2)}, u32[]{:S(2)}) collective-permute-start(bf16[1040,128]{1,0:T(8,128)(2,1)S(1)} %get-tuple-element.8.head_ref), channel_id=1, source_target_pairs={{1,0},{2,1},{3,2},{4,3},{5,4},{6,5},{7,6},{8,7},{9,8},{10,9},{11,1... | collective-permute-start | bytes 798728 | tf_op jit(solution)/shard_map/ppermute | solution.py:146
  57.4 1.3 %copy-start.1 = (bf16[1040,1024]{1,0:T(8,128)(2,1)}, bf16[1040,1024]{1,0:T(8,128)(2,1)S(1)}, u32[]{:S(2)}) copy-start(bf16[1040,1024]{1,0:T(8,128)(2,1)S(1)} %shard_map.65.weights_ref) | copy-start | bytes 6389764
  58.7 1.6 %copy-start.2 = (bf16[1040,1024]{1,0:T(8,128)(2,1)S(1)}, bf16[1040,1024]{1,0:T(8,128)(2,1)}, u32[]{:S(2)}) copy-start(bf16[1040,1024]{1,0:T(8,128)(2,1)} %copy-done.1) | copy-start | bytes 6389764

commit v2 on v1

--- a/solution.py
+++ b/solution.py
@@ -11,7 +11,7 @@
 DEGREE = 7
 NODES = DEGREE + 1
 PAD = 16
-LIMIT = 30 * 1024 * 1024
+HIGH, LOW, ONES = 0, 1, 2
 
 
 def tables():
@@ -37,16 +37,21 @@
     return dot(left[0], right[0]) + (dot(left[0], right[1]) + dot(left[1], right[0]))
 
 
-def gains_kernel(obs_ref, side_ref, head_ref, tail_ref):
+def gains_kernel(place_ref, obs_ref, values_ref, weights_ref, counts_ref, head_ref, tail_ref):
     members, own = obs_ref.shape
     half = own // 2
+    region = place_ref[0]
+    lanes = lax.broadcasted_iota(jnp.int32, counts_ref.shape, 1)
+    count = jnp.sum(jnp.where(lanes == region, counts_ref[...], 0), axis=1, keepdims=True)
+    sites = lax.broadcasted_iota(jnp.int32, (1, half), 1)
     for part, out in ((0, head_ref), (1, tail_ref)):
-        columns = slice(part * half, (part + 1) * half)
-        full = obs_ref[:, columns].astype(jnp.float32)
+        row = pl.ds(2 * region + part, 1)
+        mask = jnp.where(sites + part * half < count, 1.0, 0.0)
+        root = jnp.sqrt(weights_ref[row, :] * mask)
+        full = obs_ref[:, part * half : (part + 1) * half].astype(jnp.float32)
         centre = jnp.sum(full, axis=0, keepdims=True) * (1.0 / members)
-        root = side_ref[0:1, columns]
         out[0:members, :] = ((full - centre) * root).astype(jnp.bfloat16)
-        innov = root * (side_ref[1:2, columns] - centre)
+        innov = root * (values_ref[row, :] - centre)
         out[members:, :] = jnp.broadcast_to(innov, (PAD, half)).astype(jnp.bfloat16)
 
 
@@ -93,71 +98,107 @@
     shift = split(mean_weights * (1.0 / (members - 1)))
     turned_now = turned[...]
     rows_shift = dot(shift[0], turned_now) + dot(shift[1], turned_now)
-    high, low = split(rows_shift)
-    out_ref[members:, :] = jnp.concatenate([high[: PAD // 2], low[: PAD // 2]], axis=0)
+    high, low = split(rows_shift[0:1, :])
+    extra = lax.broadcasted_iota(jnp.int32, (PAD, members), 0)
+    high, low = (jnp.broadcast_to(row.astype(jnp.float32), (PAD, members)) for row in (high, low))
+    ones = jnp.where(extra == ONES, 1.0, 0.0)
+    below = jnp.where(extra == HIGH, high, jnp.where(extra == LOW, low, ones))
+    out_ref[members:, 0:members] = below.astype(jnp.bfloat16)
     reduced = (dot(root[0], turned_now) + dot(root[1], turned_now)).astype(jnp.bfloat16)
-    out_ref[0:members, :] = (dot(gains[...], reduced) * (1.0 / (members - 1))).astype(jnp.bfloat16)
-
-
-def apply_kernel(state_ref, weights_ref, out_ref, spread):
-    members = state_ref.shape[0]
-    total = jnp.sum(state_ref[...].astype(jnp.float32), axis=0, keepdims=True)
-    centre = total * (1.0 / members)
-    spread[...] = (state_ref[...].astype(jnp.float32) - centre).astype(jnp.bfloat16)
-    shifts = dot(weights_ref[members:, :], spread[...])
-    shift = shifts[0:1, :] + shifts[PAD // 2 : PAD // 2 + 1, :]
+    out_ref[0:members, 0:members] = (dot(gains[...], reduced) * (1.0 / (members - 1))).astype(jnp.bfloat16)
+    high, low = split(dot(out_ref[:, 0:members], jnp.ones((members, 128), jnp.bfloat16)))
+    lanes = lax.broadcasted_iota(jnp.int32, high.shape, 1)
+    high, low = high.astype(jnp.float32), low.astype(jnp.float32)
+    sums = jnp.where(lanes < 2, high, jnp.where(lanes == 2, low, 0.0))
+    out_ref[:, members:] = sums.astype(jnp.bfloat16)
+
+
+def apply_kernel(state_ref, weights_ref, out_ref):
+    members, columns = state_ref.shape
+    state = state_ref[...]
+    below = dot(weights_ref[members:, 0:members], state)
+    high, low = split(below[ONES : ONES + 1, :] * (-1.0 / members))
+    rows = lax.broadcasted_iota(jnp.int32, (128, columns), 0)
+    high, low = high.astype(jnp.float32), low.astype(jnp.float32)
+    centre = jnp.where(rows == 1, low, jnp.where(rows < 3, high, 0.0)).astype(jnp.bfloat16)
+    below = below + dot(weights_ref[members:, members:], centre)
+    shift = below[HIGH : HIGH + 1, :] + below[LOW : LOW + 1, :]
     step = 256
     for start in range(0, members, step):
         block = slice(start, start + step)
-        update = dot(weights_ref[block, :], spread[...])
+        update = dot(weights_ref[block, 0:members], state) + dot(weights_ref[block, members:], centre)
         out_ref[block, :] = (state_ref[block, :].astype(jnp.float32) + shift + update).astype(jnp.bfloat16)
 
 
-def call(kernel, out_shape, scratch, flops, nbytes, *args):
+def gather_kernel(array_ref, out_ref, done):
+    count, _, width = out_ref.shape
+    copies = [
+        pltpu.make_async_copy(array_ref.at[:, pl.ds(k * width, width)], out_ref.at[k], done.at[k])
+        for k in range(count)
+    ]
+    for copy in copies:
+        copy.start()
+    for copy in copies:
+        copy.wait()
+
+
+VMEM = pl.BlockSpec(memory_space=pltpu.VMEM)
+SMEM = pl.BlockSpec(memory_space=pltpu.SMEM)
+HBM = pl.BlockSpec(memory_space=pltpu.HBM)
+ANY = pl.BlockSpec(memory_space=pl.ANY)
+
+
+def struct(shape):
+    return jax.ShapeDtypeStruct(shape[1:], shape[0])
+
+
+def call(kernel, args, specs, outs, out_specs, scratch=(), flops=10**6, nbytes=10**6, mib=8):
     return pl.pallas_call(
         kernel,
-        out_shape=out_shape,
-        in_specs=[pl.BlockSpec(memory_space=pltpu.VMEM)] * len(args),
-        out_specs=jax.tree.map(lambda _: pl.BlockSpec(memory_space=pltpu.VMEM), out_shape),
-        scratch_shapes=scratch,
-        compiler_params=pltpu.CompilerParams(vmem_limit_bytes=LIMIT),
+        out_shape=jax.tree.map(struct, outs, is_leaf=lambda x: isinstance(x, tuple)),
+        in_specs=specs,
+        out_specs=out_specs,
+        scratch_shapes=list(scratch),
+        compiler_params=pltpu.CompilerParams(vmem_limit_bytes=mib * 1024 * 1024),
         cost_estimate=pl.CostEstimate(flops=flops, bytes_accessed=nbytes, transcendentals=0),
     )(*args)
 
 
 def on_device(state, obs_ens, obs_values, obs_weight, counts):
-    mem_index = lax.axis_index("mem")
-    own = obs_ens.shape[1] // lax.axis_size("mem")
+    mem_index = lax.axis_index("mem").astype(jnp.int32).reshape(1)
+    devices = lax.axis_size("mem")
+    patches = lax.axis_size("patch")
+    share = obs_ens.shape[0]
+    own = obs_ens.shape[1] // devices
     half = own // 2
-    patches = lax.axis_size("patch")
-    region_obs = lax.all_to_all(obs_ens, "mem", split_axis=1, concat_axis=0, tiled=True)
+    bf16 = jnp.bfloat16
+
+    blocks = call(
+        gather_kernel, (pltpu.with_memory_space_constraint(obs_ens, pltpu.HBM),), [HBM], (bf16, devices, share, own), ANY,
+        [pltpu.SemaphoreType.DMA((devices,))],
+    )
+    region_obs = lax.all_to_all(blocks, "mem", split_axis=0, concat_axis=0, tiled=True)
+    region_obs = region_obs.reshape(devices * share, own)
     region_state = lax.all_to_all(state, "mem", split_axis=1, concat_axis=0, tiled=True)
     members, columns = region_state.shape
 
-    values = lax.dynamic_slice_in_dim(obs_values, mem_index * own, own, 0)
-    weights = lax.dynamic_slice_in_dim(obs_weight, mem_index * own, own, 0)
-    count = lax.dynamic_slice_in_dim(counts, mem_index, 1, 0)[0]
-    mask = (jnp.arange(own, dtype=jnp.int32) < count).astype(jnp.float32)
-    side = jnp.stack([jnp.sqrt(weights * mask), values])
-
-    edge = jax.ShapeDtypeStruct((members + PAD, half), jnp.bfloat16)
-    head, tail = call(gains_kernel, (edge, edge), [], 10**6, 2 * 10**6, region_obs, side)
+    edge = (bf16, members + PAD, half)
+    head, tail = call(
+        gains_kernel,
+        (mem_index, region_obs, obs_values.reshape(-1, half), obs_weight.reshape(-1, half), counts.reshape(1, -1)),
+        [SMEM, VMEM, VMEM, VMEM, VMEM], [edge, edge], [VMEM, VMEM],
+    )
     left = lax.ppermute(tail, "patch", [(i, (i + 1) % patches) for i in range(patches)])
     right = lax.ppermute(head, "patch", [((i + 1) % patches, i) for i in range(patches)])
-    sites = 2 * own
     transform = call(
-        weights_kernel,
-        jax.ShapeDtypeStruct((members + PAD, members), jnp.bfloat16),
-        [pltpu.VMEM((members, sites), jnp.bfloat16), pltpu.VMEM((sites, members), jnp.bfloat16)],
-        7 * 10**9, 4 * 10**6,
-        left, head, tail, right, jnp.asarray(tables()),
+        weights_kernel, (left, head, tail, right, jnp.asarray(tables())), [VMEM] * 5,
+        (bf16, members + PAD, members + 128), VMEM,
+        [pltpu.VMEM((members, 2 * own), bf16), pltpu.VMEM((2 * own, members), bf16)],
+        7 * 10**9, 4 * 10**6, 24,
     )
     analysed = call(
-        apply_kernel,
-        jax.ShapeDtypeStruct((members, columns), jnp.bfloat16),
-        [pltpu.VMEM((members, columns), jnp.bfloat16)],
-        2 * 10**9, 4 * 10**6,
-        region_state, transform,
+        apply_kernel, (region_state, transform), [VMEM] * 2, (bf16, members, columns), VMEM,
+        (), 10**9, 4 * 10**6, 8,
     )
     return lax.all_to_all(analysed, "mem", split_axis=0, concat_axis=1, tiled=True)
 

time: 101 us -> 113 us (1.12)
  the two profiles are of different devices: /device:TPU:209 before, /device:TPU:450 now
where the time goes in v2:
time: 113 us; the launch traced here: 112 us
  blocking collectives  32.1 us (28%)
  waiting for transfers between devices  31.5 us (28%)
  Pallas kernels  28.5 us (25%)
  starting transfers between devices  17.7 us (16%)
  local copies, waits for them, and re-layouts  2.21 us (2%)
    all_to_all x1, blocking collectives, on_device(): lax.all_to_all(analysed, 'mem', split_axis=0, concat_axis=1, tiled=True)  32.1 us
    pallas_call x4, Pallas kernels, call(): pl.pallas_call(kernel, out_shape=jax.tree.map(struct, outs, is_leaf=lambd...  28.5 us
    all_to_all x1, waiting for transfers between devices, on_device(): lax.all_to_all(blocks, 'mem', split_axis=0, concat_axis=0, tiled=True)  15.7 us
    all_to_all x1, waiting for transfers between devices, on_device(): lax.all_to_all(state, 'mem', split_axis=1, concat_axis=0, tiled=True)  11.7 us
    all_to_all x1, starting transfers between devices, on_device(): lax.all_to_all(blocks, 'mem', split_axis=0, concat_axis=0, tiled=True)  10.4 us
    all_to_all x1, starting transfers between devices, on_device(): lax.all_to_all(state, 'mem', split_axis=1, concat_axis=0, tiled=True)  5.57 us
    ppermute x1, waiting for transfers between devices, on_device(): lax.ppermute(tail, 'patch', [(i, (i + 1) % patches) for i in range(patche...  4.09 us
  transfers between devices with their start and end apart: 4, of which 3 were waited for; matrix products, arithmetic and copies ran while one was open for 1% of the time, Pallas kernels for 8%

profile of v2, /device:TPU:450, one launch (start us, length us, event | category | flops | bytes accessed | tf_op | source)
XLA Modules:
  0.0 112.2 jit_solution(16292531141656502785)
XLA Ops:
  0.0 17.3 %shard_map.64 = bf16[32,32,256]{2,1,0:T(8,128)(2,1)} custom-call(bf16[32,8192]{1,0:T(8,128)(2,1)} %array_ref.1), custom_call_target="tpu_custom_call" | custom-call | flops 1000000 | bytes 1000000 | tf_op jit(solution)/shard_map/pallas_call | solution.py:156
  17.3 0.0 copy-start
  17.3 0.0 copy-start.1
  17.3 0.0 copy-start.2
  17.3 10.4 %all-to-all-start.1 = ((bf16[32,32,256]{2,1,0:T(8,128)(2,1)}), bf16[32,32,256]{2,1,0:T(8,128)(2,1)S(1)}, u32[]{:S(2)}, u32[]{:S(2)}) async-start(bf16[32,32,256]{2,1,0:T(8,128)(2,1)} %shard_map.64), calls=%async_computation.1 | async-start | bytes 1048576 | tf_op jit(solution)/shard_map/all_to_all | solution.py:180
  27.7 0.0 copy-done.4
  27.7 0.0 copy-start.3
  27.7 1.1 copy.12
  28.8 15.7 %all-to-all-done.1 = bf16[32,32,256]{2,1,0:T(8,128)(2,1)S(1)} async-done(((bf16[32,32,256]{2,1,0:T(8,128)(2,1)}), bf16[32,32,256]{2,1,0:T(8,128)(2,1)S(1)}, u32[]{:S(2)}, u32[]{:S(2)}) %all-to-all-start.1) | async-done | bytes 524320 | tf_op jit(solution)/shard_map/all_to_all | solution.py:180
  44.5 5.6 %all-to-all-start = ((bf16[32,32,512]{2,0,1:T(8,128)(2,1)}), bf16[32,32,512]{2,0,1:T(8,128)(2,1)S(1)}, u32[]{:S(2)}, u32[]{:S(2)}) async-start(bf16[32,32,512]{2,0,1:T(8,128)(2,1)} %bitcast.15), calls=%async_computation | async-start | bytes 2097152 | tf_op jit(solution)/shard_map/all_to_all | solution.py:182
  50.1 0.0 copy-done
  50.1 0.0 copy-done.1
  50.1 0.0 copy-done.2
  50.2 0.3 shard_map.65
  50.5 0.0 collective-permute-start
  50.5 1.7 %collective-permute-start.1 = (bf16[1040,128]{1,0:T(8,128)(2,1)S(1)}, bf16[1040,128]{1,0:T(8,128)(2,1)S(1)}, u32[]{:S(2)}, u32[]{:S(2)}) collective-permute-start(bf16[1040,128]{1,0:T(8,128)(2,1)S(1)} %get-tuple-element.8.head_ref), channel_id=1, source_target_pairs={{1,0},{2,1},{3,2},{4,3},{5,4},{6,5},{7,6},{8,7},{9,8},{10,9},{11,1... | collective-permute-start | bytes 798728 | tf_op jit(solution)/shard_map/ppermute | solution.py:192
  52.3 4.1 %collective-permute-done.left_ref = bf16[1040,128]{1,0:T(8,128)(2,1)S(1)} collective-permute-done((bf16[1040,128]{1,0:T(8,128)(2,1)S(1)}, bf16[1040,128]{1,0:T(8,128)(2,1)S(1)}, u32[]{:S(2)}, u32[]{:S(2)}) %collective-permute-start) | collective-permute-done | bytes 266272 | tf_op jit(solution)/shard_map/ppermute | solution.py:191
  56.4 0.0 collective-permute-done.1.right_ref
  56.4 0.0 copy-done.3
  56.4 9.2 %shard_map.66.weights_ref = bf16[1040,1152]{1,0:T(8,128)(2,1)S(1)} custom-call(bf16[1040,128]{1,0:T(8,128)(2,1)S(1)} %collective-permute-done.left_ref, bf16[1040,128]{1,0:T(8,128)(2,1)S(1)} %get-tuple-element.8.head_ref, bf16[1040,128]{1,0:T(8,128)(2,1)S(1)} %get-tuple-element.7.tail_ref, bf16[1040,128]{1,0:T(8,128)(2,1)S(1)} %collective-permute-done.1.right_ref, ...), custom_call_target="tpu_custom_call" | custom-call | flops 7000000000 | bytes 4000000 | tf_op jit(solution)/shard_map/pallas_call | solution.py:156
  65.5 11.7 %all-to-all-done = bf16[32,32,512]{2,0,1:T(8,128)(2,1)S(1)} async-done(((bf16[32,32,512]{2,0,1:T(8,128)(2,1)}), bf16[32,32,512]{2,0,1:T(8,128)(2,1)S(1)}, u32[]{:S(2)}, u32[]{:S(2)}) %all-to-all-start) | async-done | bytes 1048608 | tf_op jit(solution)/shard_map/all_to_all | solution.py:182
  77.3 1.7 %shard_map.67 = bf16[1024,512]{1,0:T(8,128)(2,1)S(1)} custom-call(bf16[1024,512]{1,0:T(8,128)(2,1)S(1)} %bitcast.16, bf16[1040,1152]{1,0:T(8,128)(2,1)S(1)} %shard_map.66.weights_ref), custom_call_target="tpu_custom_call" | custom-call | flops 1000000000 | bytes 4000000 | tf_op jit(solution)/shard_map/pallas_call | solution.py:156
  79.0 32.1 %all_to_all.43 = bf16[32,32,512]{2,1,0:T(8,128)(2,1)S(1)} all-to-all(bf16[32,32,512]{2,1,0:T(8,128)(2,1)S(1)} %bitcast.17), channel_id=1, replica_groups=mesh['mem'=32,'patch'=24] {'mem'}, dimensions={0} | all-to-all | bytes 2097152 | tf_op jit(solution)/shard_map/all_to_all | solution.py:203
  111.1 1.1 copy.10
  (1 shorter events, 0.0 us)
Async XLA Ops:
  0.0 27.7 %copy-start.4 = (bf16[32,16384]{1,0:T(8,128)(2,1)S(1)}, bf16[32,16384]{1,0:T(8,128)(2,1)}, u32[]{:S(2)}) copy-start(bf16[32,16384]{1,0:T(8,128)(2,1)} %param.6) | copy-start | bytes 3145732
  17.3 32.8 %copy-start = (f32[8192]{0:T(1024)S(1)}, f32[8192]{0:T(1024)}, u32[]{:S(2)}) copy-start(f32[8192]{0:T(1024)} %param.8) | copy-start | bytes 98308
  17.3 32.8 %copy-start.1 = (f32[8192]{0:T(1024)S(1)}, f32[8192]{0:T(1024)}, u32[]{:S(2)}) copy-start(f32[8192]{0:T(1024)} %param.9) | copy-start | bytes 98308
  17.3 32.8 %copy-start.2 = (s32[32]{0:T(128)S(1)}, s32[32]{0:T(128)}, u32[]{:S(2)}) copy-start(s32[32]{0:T(128)} %param.10) | copy-start | bytes 388
  17.3 27.2 %all-to-all-start.1 = ((bf16[32,32,256]{2,1,0:T(8,128)(2,1)}), bf16[32,32,256]{2,1,0:T(8,128)(2,1)S(1)}, u32[]{:S(2)}, u32[]{:S(2)}) async-start(bf16[32,32,256]{2,1,0:T(8,128)(2,1)} %shard_map.64), calls=%async_computation.1 | async-start | bytes 1048576 | tf_op jit(solution)/shard_map/all_to_all | solution.py:180
  27.7 28.6 %copy-start.3 = (f32[16,128]{1,0:T(8,128)S(1)}, f32[16,128]{1,0:T(8,128)}, u32[]{:S(2)}) copy-start(f32[16,128]{1,0:T(8,128)} %constant.7.clone.table_ref) | copy-start | bytes 24580
  44.5 32.7 %all-to-all-start = ((bf16[32,32,512]{2,0,1:T(8,128)(2,1)}), bf16[32,32,512]{2,0,1:T(8,128)(2,1)S(1)}, u32[]{:S(2)}, u32[]{:S(2)}) async-start(bf16[32,32,512]{2,0,1:T(8,128)(2,1)} %bitcast.15), calls=%async_computation | async-start | bytes 2097152 | tf_op jit(solution)/shard_map/all_to_all | solution.py:182
  50.5 5.9 %collective-permute-start = (bf16[1040,128]{1,0:T(8,128)(2,1)S(1)}, bf16[1040,128]{1,0:T(8,128)(2,1)S(1)}, u32[]{:S(2)}, u32[]{:S(2)}) collective-permute-start(bf16[1040,128]{1,0:T(8,128)(2,1)S(1)} %get-tuple-element.7.tail_ref), channel_id=1, source_target_pairs={{0,1},{1,2},{2,3},{3,4},{4,5},{5,6},{6,7},{7,8},{8,9},{9,10},{10,1... | collective-permute-start | bytes 798728 | tf_op jit(solution)/shard_map/ppermute | solution.py:191
  50.5 5.8 %collective-permute-start.1 = (bf16[1040,128]{1,0:T(8,128)(2,1)S(1)}, bf16[1040,128]{1,0:T(8,128)(2,1)S(1)}, u32[]{:S(2)}, u32[]{:S(2)}) collective-permute-start(bf16[1040,128]{1,0:T(8,128)(2,1)S(1)} %get-tuple-element.8.head_ref), channel_id=1, source_target_pairs={{1,0},{2,1},{3,2},{4,3},{5,4},{6,5},{7,6},{8,7},{9,8},{10,9},{11,1... | collective-permute-start | bytes 798728 | tf_op jit(solution)/shard_map/ppermute | solution.py:192

commit v3 on v2

--- a/solution.py
+++ b/solution.py
@@ -144,7 +144,6 @@
 
 VMEM = pl.BlockSpec(memory_space=pltpu.VMEM)
 SMEM = pl.BlockSpec(memory_space=pltpu.SMEM)
-HBM = pl.BlockSpec(memory_space=pltpu.HBM)
 ANY = pl.BlockSpec(memory_space=pl.ANY)
 
 
@@ -174,7 +173,7 @@
     bf16 = jnp.bfloat16
 
     blocks = call(
-        gather_kernel, (pltpu.with_memory_space_constraint(obs_ens, pltpu.HBM),), [HBM], (bf16, devices, share, own), ANY,
+        gather_kernel, (obs_ens,), [VMEM], (bf16, devices, share, own), ANY,
         [pltpu.SemaphoreType.DMA((devices,))],
     )
     region_obs = lax.all_to_all(blocks, "mem", split_axis=0, concat_axis=0, tiled=True)

time: 113 us -> 97.4 us (0.86)
  the two profiles are of different devices: /device:TPU:450 before, /device:TPU:386 now
where the time goes in v3:
time: 97.4 us; the launch traced here: 97 us
  blocking collectives  32.1 us (33%)
  waiting for transfers between devices  31.5 us (32%)
  starting transfers between devices  17.7 us (18%)
  Pallas kernels  12.3 us (13%)
  local copies, waits for them, and re-layouts  3.25 us (3%)
    all_to_all x1, blocking collectives, on_device(): lax.all_to_all(analysed, 'mem', split_axis=0, concat_axis=1, tiled=True)  32.1 us
    all_to_all x1, waiting for transfers between devices, on_device(): lax.all_to_all(blocks, 'mem', split_axis=0, concat_axis=0, tiled=True)  15.7 us
    pallas_call x4, Pallas kernels, call(): pl.pallas_call(kernel, out_shape=jax.tree.map(struct, outs, is_leaf=lambd...  12.3 us
    all_to_all x1, waiting for transfers between devices, on_device(): lax.all_to_all(state, 'mem', split_axis=1, concat_axis=0, tiled=True)  11.7 us
    all_to_all x1, starting transfers between devices, on_device(): lax.all_to_all(blocks, 'mem', split_axis=0, concat_axis=0, tiled=True)  10.4 us
    all_to_all x1, starting transfers between devices, on_device(): lax.all_to_all(state, 'mem', split_axis=1, concat_axis=0, tiled=True)  5.57 us
    ppermute x1, waiting for transfers between devices, on_device(): lax.ppermute(tail, 'patch', [(i, (i + 1) % patches) for i in range(patche...  4.09 us
  transfers between devices with their start and end apart: 4, of which 3 were waited for; matrix products, arithmetic and copies ran while one was open for 1% of the time, Pallas kernels for 10%

profile of v3, /device:TPU:386, one launch (start us, length us, event | category | flops | bytes accessed | tf_op | source)
XLA Modules:
  0.0 97.0 jit_solution(3698382322131734171)
XLA Ops:
  0.0 1.0 %copy-done = bf16[32,8192]{1,0:T(8,128)(2,1)S(1)} copy-done((bf16[32,8192]{1,0:T(8,128)(2,1)S(1)}, bf16[32,8192]{1,0:T(8,128)(2,1)}, u32[]{:S(2)}) %copy-start) | copy-done | bytes 524312
  1.0 1.1 %shard_map.64 = bf16[32,32,256]{2,1,0:T(8,128)(2,1)} custom-call(bf16[32,8192]{1,0:T(8,128)(2,1)S(1)} %copy-done), custom_call_target="tpu_custom_call" | custom-call | flops 1000000 | bytes 1000000 | tf_op jit(solution)/shard_map/pallas_call | solution.py:155
  2.1 0.0 copy-start.1
  2.2 0.0 copy-start.2
  2.2 0.0 copy-start.3
  2.2 10.4 %all-to-all-start.1 = ((bf16[32,32,256]{2,1,0:T(8,128)(2,1)}), bf16[32,32,256]{2,1,0:T(8,128)(2,1)S(1)}, u32[]{:S(2)}, u32[]{:S(2)}) async-start(bf16[32,32,256]{2,1,0:T(8,128)(2,1)} %shard_map.64), calls=%async_computation.1 | async-start | bytes 1048576 | tf_op jit(solution)/shard_map/all_to_all | solution.py:179
  12.6 0.0 copy-done.5
  12.6 0.0 copy-start.4
  12.6 1.1 %copy.12 = bf16[4,32,8,512]{3,2,0,1:T(8,128)(2,1)} copy(bf16[4,32,8,512]{3,2,1,0:T(8,128)(2,1)S(1)} %bitcast.23) | data formatting | bytes 2097152 | tf_op jit(solution)/shard_map/all_to_all | solution.py:181
  13.7 15.7 %all-to-all-done.1 = bf16[32,32,256]{2,1,0:T(8,128)(2,1)S(1)} async-done(((bf16[32,32,256]{2,1,0:T(8,128)(2,1)}), bf16[32,32,256]{2,1,0:T(8,128)(2,1)S(1)}, u32[]{:S(2)}, u32[]{:S(2)}) %all-to-all-start.1) | async-done | bytes 524320 | tf_op jit(solution)/shard_map/all_to_all | solution.py:179
  29.4 5.6 %all-to-all-start = ((bf16[32,32,512]{2,0,1:T(8,128)(2,1)}), bf16[32,32,512]{2,0,1:T(8,128)(2,1)S(1)}, u32[]{:S(2)}, u32[]{:S(2)}) async-start(bf16[32,32,512]{2,0,1:T(8,128)(2,1)} %bitcast.15), calls=%async_computation | async-start | bytes 2097152 | tf_op jit(solution)/shard_map/all_to_all | solution.py:181
  35.0 0.0 copy-done.1
  35.0 0.0 copy-done.2
  35.0 0.0 copy-done.3
  35.0 0.3 shard_map.65
  35.4 0.0 collective-permute-start
  35.4 1.7 %collective-permute-start.1 = (bf16[1040,128]{1,0:T(8,128)(2,1)S(1)}, bf16[1040,128]{1,0:T(8,128)(2,1)S(1)}, u32[]{:S(2)}, u32[]{:S(2)}) collective-permute-start(bf16[1040,128]{1,0:T(8,128)(2,1)S(1)} %get-tuple-element.8.head_ref), channel_id=1, source_target_pairs={{1,0},{2,1},{3,2},{4,3},{5,4},{6,5},{7,6},{8,7},{9,8},{10,9},{11,1... | collective-permute-start | bytes 798728 | tf_op jit(solution)/shard_map/ppermute | solution.py:191
  37.1 4.1 %collective-permute-done.left_ref = bf16[1040,128]{1,0:T(8,128)(2,1)S(1)} collective-permute-done((bf16[1040,128]{1,0:T(8,128)(2,1)S(1)}, bf16[1040,128]{1,0:T(8,128)(2,1)S(1)}, u32[]{:S(2)}, u32[]{:S(2)}) %collective-permute-start) | collective-permute-done | bytes 266272 | tf_op jit(solution)/shard_map/ppermute | solution.py:190
  41.2 0.0 collective-permute-done.1.right_ref
  41.2 9.1 %shard_map.66.weights_ref = bf16[1040,1152]{1,0:T(8,128)(2,1)S(1)} custom-call(bf16[1040,128]{1,0:T(8,128)(2,1)S(1)} %collective-permute-done.left_ref, bf16[1040,128]{1,0:T(8,128)(2,1)S(1)} %get-tuple-element.8.head_ref, bf16[1040,128]{1,0:T(8,128)(2,1)S(1)} %get-tuple-element.7.tail_ref, bf16[1040,128]{1,0:T(8,128)(2,1)S(1)} %collective-permute-done.1.right_ref, ...), custom_call_target="tpu_custom_call" | custom-call | flops 7000000000 | bytes 4000000 | tf_op jit(solution)/shard_map/pallas_call | solution.py:155
  50.4 11.7 %all-to-all-done = bf16[32,32,512]{2,0,1:T(8,128)(2,1)S(1)} async-done(((bf16[32,32,512]{2,0,1:T(8,128)(2,1)}), bf16[32,32,512]{2,0,1:T(8,128)(2,1)S(1)}, u32[]{:S(2)}, u32[]{:S(2)}) %all-to-all-start) | async-done | bytes 1048608 | tf_op jit(solution)/shard_map/all_to_all | solution.py:181
  62.1 1.7 %shard_map.67 = bf16[1024,512]{1,0:T(8,128)(2,1)S(1)} custom-call(bf16[1024,512]{1,0:T(8,128)(2,1)S(1)} %bitcast.16, bf16[1040,1152]{1,0:T(8,128)(2,1)S(1)} %shard_map.66.weights_ref), custom_call_target="tpu_custom_call" | custom-call | flops 1000000000 | bytes 4000000 | tf_op jit(solution)/shard_map/pallas_call | solution.py:155
  63.9 32.1 %all_to_all.43 = bf16[32,32,512]{2,1,0:T(8,128)(2,1)S(1)} all-to-all(bf16[32,32,512]{2,1,0:T(8,128)(2,1)S(1)} %bitcast.17), channel_id=1, replica_groups=mesh['mem'=32,'patch'=24] {'mem'}, dimensions={0} | all-to-all | bytes 2097152 | tf_op jit(solution)/shard_map/all_to_all | solution.py:202
  96.0 1.1 %copy.10 = bf16[32,4,8,512]{3,2,0,1:T(8,128)(2,1)} copy(bf16[32,4,8,512]{3,2,1,0:T(8,128)(2,1)S(1)} %bitcast.22) | data formatting | bytes 2097152 | tf_op jit(solution)/shard_map/all_to_all | solution.py:202
  (3 shorter events, 0.0 us)
Async XLA Ops:
  0.0 1.0 %copy-start = (bf16[32,8192]{1,0:T(8,128)(2,1)S(1)}, bf16[32,8192]{1,0:T(8,128)(2,1)}, u32[]{:S(2)}) copy-start(bf16[32,8192]{1,0:T(8,128)(2,1)} %array_ref.1) | copy-start | bytes 1572868
  1.0 11.5 %copy-start.5 = (bf16[32,16384]{1,0:T(8,128)(2,1)S(1)}, bf16[32,16384]{1,0:T(8,128)(2,1)}, u32[]{:S(2)}) copy-start(bf16[32,16384]{1,0:T(8,128)(2,1)} %param.6) | copy-start | bytes 3145732
  2.1 32.9 %copy-start.1 = (f32[8192]{0:T(1024)S(1)}, f32[8192]{0:T(1024)}, u32[]{:S(2)}) copy-start(f32[8192]{0:T(1024)} %param.8) | copy-start | bytes 98308
  2.2 32.9 %copy-start.2 = (f32[8192]{0:T(1024)S(1)}, f32[8192]{0:T(1024)}, u32[]{:S(2)}) copy-start(f32[8192]{0:T(1024)} %param.9) | copy-start | bytes 98308
  2.2 32.8 %copy-start.3 = (s32[32]{0:T(128)S(1)}, s32[32]{0:T(128)}, u32[]{:S(2)}) copy-start(s32[32]{0:T(128)} %param.10) | copy-start | bytes 388
  2.2 27.2 %all-to-all-start.1 = ((bf16[32,32,256]{2,1,0:T(8,128)(2,1)}), bf16[32,32,256]{2,1,0:T(8,128)(2,1)S(1)}, u32[]{:S(2)}, u32[]{:S(2)}) async-start(bf16[32,32,256]{2,1,0:T(8,128)(2,1)} %shard_map.64), calls=%async_computation.1 | async-start | bytes 1048576 | tf_op jit(solution)/shard_map/all_to_all | solution.py:179
  12.6 28.6 %copy-start.4 = (f32[16,128]{1,0:T(8,128)S(1)}, f32[16,128]{1,0:T(8,128)}, u32[]{:S(2)}) copy-start(f32[16,128]{1,0:T(8,128)} %constant.7.clone.table_ref) | copy-start | bytes 24580
  29.4 32.7 %all-to-all-start = ((bf16[32,32,512]{2,0,1:T(8,128)(2,1)}), bf16[32,32,512]{2,0,1:T(8,128)(2,1)S(1)}, u32[]{:S(2)}, u32[]{:S(2)}) async-start(bf16[32,32,512]{2,0,1:T(8,128)(2,1)} %bitcast.15), calls=%async_computation | async-start | bytes 2097152 | tf_op jit(solution)/shard_map/all_to_all | solution.py:181
  35.4 5.9 %collective-permute-start = (bf16[1040,128]{1,0:T(8,128)(2,1)S(1)}, bf16[1040,128]{1,0:T(8,128)(2,1)S(1)}, u32[]{:S(2)}, u32[]{:S(2)}) collective-permute-start(bf16[1040,128]{1,0:T(8,128)(2,1)S(1)} %get-tuple-element.7.tail_ref), channel_id=1, source_target_pairs={{0,1},{1,2},{2,3},{3,4},{4,5},{5,6},{6,7},{7,8},{8,9},{9,10},{10,1... | collective-permute-start | bytes 798728 | tf_op jit(solution)/shard_map/ppermute | solution.py:190
  35.4 5.8 %collective-permute-start.1 = (bf16[1040,128]{1,0:T(8,128)(2,1)S(1)}, bf16[1040,128]{1,0:T(8,128)(2,1)S(1)}, u32[]{:S(2)}, u32[]{:S(2)}) collective-permute-start(bf16[1040,128]{1,0:T(8,128)(2,1)S(1)} %get-tuple-element.8.head_ref), channel_id=1, source_target_pairs={{1,0},{2,1},{3,2},{4,3},{5,4},{6,5},{7,6},{8,7},{9,8},{10,9},{11,1... | collective-permute-start | bytes 798728 | tf_op jit(solution)/shard_map/ppermute | solution.py:191

commit v4 on v3

--- a/solution.py
+++ b/solution.py
@@ -11,7 +11,6 @@
 DEGREE = 7
 NODES = DEGREE + 1
 PAD = 16
-HIGH, LOW, ONES = 0, 1, 2
 
 
 def tables():
@@ -87,46 +86,39 @@
     t4 = 2.0 * product(t2_parts, t2_parts) - eye
     t4_parts = split(t4)
 
-    def polynomial(c):
+    def split_polynomial(c):
         inner = c[5] * t1 + c[6] * t2 + c[7] * t3
         outer = c[0] * eye + (c[1] - c[7]) * t1 + (c[2] - c[6]) * t2 + (c[3] - c[5]) * t3 + c[4] * t4
-        return outer + 2.0 * product(split(inner), t4_parts)
-
-    root = split(polynomial(a))
-    inverse = split(polynomial(e))
-    mean_weights = dot(innov, inverse[0]) + dot(innov, inverse[1])
-    shift = split(mean_weights * (1.0 / (members - 1)))
-    turned_now = turned[...]
-    rows_shift = dot(shift[0], turned_now) + dot(shift[1], turned_now)
-    high, low = split(rows_shift[0:1, :])
-    extra = lax.broadcasted_iota(jnp.int32, (PAD, members), 0)
-    high, low = (jnp.broadcast_to(row.astype(jnp.float32), (PAD, members)) for row in (high, low))
-    ones = jnp.where(extra == ONES, 1.0, 0.0)
-    below = jnp.where(extra == HIGH, high, jnp.where(extra == LOW, low, ones))
-    out_ref[members:, 0:members] = below.astype(jnp.bfloat16)
-    reduced = (dot(root[0], turned_now) + dot(root[1], turned_now)).astype(jnp.bfloat16)
-    out_ref[0:members, 0:members] = (dot(gains[...], reduced) * (1.0 / (members - 1))).astype(jnp.bfloat16)
-    high, low = split(dot(out_ref[:, 0:members], jnp.ones((members, 128), jnp.bfloat16)))
-    lanes = lax.broadcasted_iota(jnp.int32, high.shape, 1)
-    high, low = high.astype(jnp.float32), low.astype(jnp.float32)
-    sums = jnp.where(lanes < 2, high, jnp.where(lanes == 2, low, 0.0))
-    out_ref[:, members:] = sums.astype(jnp.bfloat16)
+        return split(inner), outer
+
+    inner, outer = split_polynomial(e)
+    outer = split(outer)
+    row = dot(innov, outer[0]) + dot(innov, outer[1])
+    row = row + 2.0 * product(split(dot(innov, inner[0]) + dot(innov, inner[1])), t4_parts)
+    shift = split(row * (1.0 / (members - 1)))
+    across = turned[...]
+    row = dot(shift[0], across) + dot(shift[1], across)
+    row = row - jnp.sum(row, axis=1, keepdims=True) * (1.0 / members)
+    high, low = (part.astype(jnp.float32) for part in split(row))
+    below = jnp.where(lax.broadcasted_iota(jnp.int32, row.shape, 0) < PAD // 2, high, low)
+    out_ref[members:, :] = below.astype(jnp.bfloat16)
+
+    inner, outer = split_polynomial(a)
+    root = split(outer + 2.0 * product(inner, t4_parts))
+    reduced = dot(root[0], across) + dot(root[1], across)
+    reduced = reduced - jnp.sum(reduced, axis=1, keepdims=True) * (1.0 / members)
+    update = dot(gains[...], reduced.astype(jnp.bfloat16))
+    out_ref[0:members, :] = (update * (1.0 / (members - 1))).astype(jnp.bfloat16)
 
 
 def apply_kernel(state_ref, weights_ref, out_ref):
-    members, columns = state_ref.shape
-    state = state_ref[...]
-    below = dot(weights_ref[members:, 0:members], state)
-    high, low = split(below[ONES : ONES + 1, :] * (-1.0 / members))
-    rows = lax.broadcasted_iota(jnp.int32, (128, columns), 0)
-    high, low = high.astype(jnp.float32), low.astype(jnp.float32)
-    centre = jnp.where(rows == 1, low, jnp.where(rows < 3, high, 0.0)).astype(jnp.bfloat16)
-    below = below + dot(weights_ref[members:, members:], centre)
-    shift = below[HIGH : HIGH + 1, :] + below[LOW : LOW + 1, :]
+    members = state_ref.shape[0]
+    below = dot(weights_ref[members:, :], state_ref[...])
+    shift = below[0:1, :] + below[PAD // 2 : PAD // 2 + 1, :]
     step = 256
     for start in range(0, members, step):
         block = slice(start, start + step)
-        update = dot(weights_ref[block, 0:members], state) + dot(weights_ref[block, members:], centre)
+        update = dot(weights_ref[block, :], state_ref[...])
         out_ref[block, :] = (state_ref[block, :].astype(jnp.float32) + shift + update).astype(jnp.bfloat16)
 
 
@@ -191,7 +183,7 @@
     right = lax.ppermute(head, "patch", [((i + 1) % patches, i) for i in range(patches)])
     transform = call(
         weights_kernel, (left, head, tail, right, jnp.asarray(tables())), [VMEM] * 5,
-        (bf16, members + PAD, members + 128), VMEM,
+        (bf16, members + PAD, members), VMEM,
         [pltpu.VMEM((members, 2 * own), bf16), pltpu.VMEM((2 * own, members), bf16)],
         7 * 10**9, 4 * 10**6, 24,
     )

time: 97.4 us -> 96.9 us (level)
  the two profiles are of different devices: /device:TPU:386 before, /device:TPU:322 now
where the time goes in v4:
time: 96.9 us; the launch traced here: 96.5 us
  waiting for transfers between devices  32.3 us (33%)
  blocking collectives  32.1 us (33%)
  starting transfers between devices  17.6 us (18%)
  Pallas kernels  11.2 us (12%)
  local copies, waits for them, and re-layouts  3.25 us (3%)
    all_to_all x1, blocking collectives, on_device(): lax.all_to_all(analysed, 'mem', split_axis=0, concat_axis=1, tiled=True)  32.1 us
    all_to_all x1, waiting for transfers between devices, on_device(): lax.all_to_all(blocks, 'mem', split_axis=0, concat_axis=0, tiled=True)  15.7 us
    all_to_all x1, waiting for transfers between devices, on_device(): lax.all_to_all(state, 'mem', split_axis=1, concat_axis=0, tiled=True)  12.5 us
    pallas_call x4, Pallas kernels, call(): pl.pallas_call(kernel, out_shape=jax.tree.map(struct, outs, is_leaf=lambd...  11.2 us
    all_to_all x1, starting transfers between devices, on_device(): lax.all_to_all(blocks, 'mem', split_axis=0, concat_axis=0, tiled=True)  10.3 us
    all_to_all x1, starting transfers between devices, on_device(): lax.all_to_all(state, 'mem', split_axis=1, concat_axis=0, tiled=True)  5.57 us
    ppermute x1, waiting for transfers between devices, on_device(): lax.ppermute(tail, 'patch', [(i, (i + 1) % patches) for i in range(patche...  4.09 us
  transfers between devices with their start and end apart: 4, of which 3 were waited for; matrix products, arithmetic and copies ran while one was open for 1% of the time, Pallas kernels for 9%

profile of v4, /device:TPU:322, one launch (start us, length us, event | category | flops | bytes accessed | tf_op | source)
XLA Modules:
  0.0 96.5 jit_solution(3565187348559984790)
XLA Ops:
  0.0 1.0 %copy-done = bf16[32,8192]{1,0:T(8,128)(2,1)S(1)} copy-done((bf16[32,8192]{1,0:T(8,128)(2,1)S(1)}, bf16[32,8192]{1,0:T(8,128)(2,1)}, u32[]{:S(2)}) %copy-start) | copy-done | bytes 524312
  1.0 1.1 %shard_map.64 = bf16[32,32,256]{2,1,0:T(8,128)(2,1)} custom-call(bf16[32,8192]{1,0:T(8,128)(2,1)S(1)} %copy-done), custom_call_target="tpu_custom_call" | custom-call | flops 1000000 | bytes 1000000 | tf_op jit(solution)/shard_map/pallas_call | solution.py:147
  2.1 10.3 %all-to-all-start.1 = ((bf16[32,32,256]{2,1,0:T(8,128)(2,1)}), bf16[32,32,256]{2,1,0:T(8,128)(2,1)S(1)}, u32[]{:S(2)}, u32[]{:S(2)}) async-start(bf16[32,32,256]{2,1,0:T(8,128)(2,1)} %shard_map.64), calls=%async_computation.1 | async-start | bytes 1048576 | tf_op jit(solution)/shard_map/all_to_all | solution.py:171
  12.4 0.0 copy-start.1
  12.4 0.0 copy-start.2
  12.4 0.0 copy-start.3
  12.4 0.0 copy-done.5
  12.5 0.0 copy-start.4
  12.5 1.1 %copy.12 = bf16[4,32,8,512]{3,2,0,1:T(8,128)(2,1)} copy(bf16[4,32,8,512]{3,2,1,0:T(8,128)(2,1)S(1)} %bitcast.23) | data formatting | bytes 2097152 | tf_op jit(solution)/shard_map/all_to_all | solution.py:173
  13.6 15.7 %all-to-all-done.1 = bf16[32,32,256]{2,1,0:T(8,128)(2,1)S(1)} async-done(((bf16[32,32,256]{2,1,0:T(8,128)(2,1)}), bf16[32,32,256]{2,1,0:T(8,128)(2,1)S(1)}, u32[]{:S(2)}, u32[]{:S(2)}) %all-to-all-start.1) | async-done | bytes 524320 | tf_op jit(solution)/shard_map/all_to_all | solution.py:171
  29.2 5.6 %all-to-all-start = ((bf16[32,32,512]{2,0,1:T(8,128)(2,1)}), bf16[32,32,512]{2,0,1:T(8,128)(2,1)S(1)}, u32[]{:S(2)}, u32[]{:S(2)}) async-start(bf16[32,32,512]{2,0,1:T(8,128)(2,1)} %bitcast.15), calls=%async_computation | async-start | bytes 2097152 | tf_op jit(solution)/shard_map/all_to_all | solution.py:173
  34.8 0.0 copy-done.1
  34.8 0.0 copy-done.2
  34.8 0.0 copy-done.3
  34.8 0.3 shard_map.65
  35.2 0.0 collective-permute-start
  35.2 1.7 %collective-permute-start.1 = (bf16[1040,128]{1,0:T(8,128)(2,1)S(1)}, bf16[1040,128]{1,0:T(8,128)(2,1)S(1)}, u32[]{:S(2)}, u32[]{:S(2)}) collective-permute-start(bf16[1040,128]{1,0:T(8,128)(2,1)S(1)} %get-tuple-element.8.head_ref), channel_id=1, source_target_pairs={{1,0},{2,1},{3,2},{4,3},{5,4},{6,5},{7,6},{8,7},{9,8},{10,9},{11,1... | collective-permute-start | bytes 798728 | tf_op jit(solution)/shard_map/ppermute | solution.py:183
  37.0 4.1 %collective-permute-done.left_ref = bf16[1040,128]{1,0:T(8,128)(2,1)S(1)} collective-permute-done((bf16[1040,128]{1,0:T(8,128)(2,1)S(1)}, bf16[1040,128]{1,0:T(8,128)(2,1)S(1)}, u32[]{:S(2)}, u32[]{:S(2)}) %collective-permute-start) | collective-permute-done | bytes 266272 | tf_op jit(solution)/shard_map/ppermute | solution.py:182
  41.1 0.0 collective-permute-done.1.right_ref
  41.1 8.4 %shard_map.66.weights_ref = bf16[1040,1024]{1,0:T(8,128)(2,1)S(1)} custom-call(bf16[1040,128]{1,0:T(8,128)(2,1)S(1)} %collective-permute-done.left_ref, bf16[1040,128]{1,0:T(8,128)(2,1)S(1)} %get-tuple-element.8.head_ref, bf16[1040,128]{1,0:T(8,128)(2,1)S(1)} %get-tuple-element.7.tail_ref, bf16[1040,128]{1,0:T(8,128)(2,1)S(1)} %collective-permute-done.1.right_ref, ...), custom_call_target="tpu_custom_call" | custom-call | flops 7000000000 | bytes 4000000 | tf_op jit(solution)/shard_map/pallas_call | solution.py:147
  49.5 12.5 %all-to-all-done = bf16[32,32,512]{2,0,1:T(8,128)(2,1)S(1)} async-done(((bf16[32,32,512]{2,0,1:T(8,128)(2,1)}), bf16[32,32,512]{2,0,1:T(8,128)(2,1)S(1)}, u32[]{:S(2)}, u32[]{:S(2)}) %all-to-all-start) | async-done | bytes 1048608 | tf_op jit(solution)/shard_map/all_to_all | solution.py:173
  62.0 1.4 %shard_map.67 = bf16[1024,512]{1,0:T(8,128)(2,1)S(1)} custom-call(bf16[1024,512]{1,0:T(8,128)(2,1)S(1)} %bitcast.16, bf16[1040,1024]{1,0:T(8,128)(2,1)S(1)} %shard_map.66.weights_ref), custom_call_target="tpu_custom_call" | custom-call | flops 1000000000 | bytes 4000000 | tf_op jit(solution)/shard_map/pallas_call | solution.py:147
  63.4 32.1 %all_to_all.43 = bf16[32,32,512]{2,1,0:T(8,128)(2,1)S(1)} all-to-all(bf16[32,32,512]{2,1,0:T(8,128)(2,1)S(1)} %bitcast.17), channel_id=1, replica_groups=mesh['mem'=32,'patch'=24] {'mem'}, dimensions={0} | all-to-all | bytes 2097152 | tf_op jit(solution)/shard_map/all_to_all | solution.py:194
  95.4 1.1 %copy.10 = bf16[32,4,8,512]{3,2,0,1:T(8,128)(2,1)} copy(bf16[32,4,8,512]{3,2,1,0:T(8,128)(2,1)S(1)} %bitcast.22) | data formatting | bytes 2097152 | tf_op jit(solution)/shard_map/all_to_all | solution.py:194
  (3 shorter events, 0.0 us)
Async XLA Ops:
  0.0 1.0 %copy-start = (bf16[32,8192]{1,0:T(8,128)(2,1)S(1)}, bf16[32,8192]{1,0:T(8,128)(2,1)}, u32[]{:S(2)}) copy-start(bf16[32,8192]{1,0:T(8,128)(2,1)} %array_ref.1) | copy-start | bytes 1572868
  1.0 11.4 %copy-start.5 = (bf16[32,16384]{1,0:T(8,128)(2,1)S(1)}, bf16[32,16384]{1,0:T(8,128)(2,1)}, u32[]{:S(2)}) copy-start(bf16[32,16384]{1,0:T(8,128)(2,1)} %param.6) | copy-start | bytes 3145732
  2.1 27.1 %all-to-all-start.1 = ((bf16[32,32,256]{2,1,0:T(8,128)(2,1)}), bf16[32,32,256]{2,1,0:T(8,128)(2,1)S(1)}, u32[]{:S(2)}, u32[]{:S(2)}) async-start(bf16[32,32,256]{2,1,0:T(8,128)(2,1)} %shard_map.64), calls=%async_computation.1 | async-start | bytes 1048576 | tf_op jit(solution)/shard_map/all_to_all | solution.py:171
  12.4 22.4 %copy-start.1 = (f32[8192]{0:T(1024)S(1)}, f32[8192]{0:T(1024)}, u32[]{:S(2)}) copy-start(f32[8192]{0:T(1024)} %param.8) | copy-start | bytes 98308
  12.4 22.4 %copy-start.2 = (f32[8192]{0:T(1024)S(1)}, f32[8192]{0:T(1024)}, u32[]{:S(2)}) copy-start(f32[8192]{0:T(1024)} %param.9) | copy-start | bytes 98308
  12.4 22.4 %copy-start.3 = (s32[32]{0:T(128)S(1)}, s32[32]{0:T(128)}, u32[]{:S(2)}) copy-start(s32[32]{0:T(128)} %param.10) | copy-start | bytes 388
  12.5 28.6 %copy-start.4 = (f32[16,128]{1,0:T(8,128)S(1)}, f32[16,128]{1,0:T(8,128)}, u32[]{:S(2)}) copy-start(f32[16,128]{1,0:T(8,128)} %constant.7.clone.table_ref) | copy-start | bytes 24580
  29.2 32.7 %all-to-all-start = ((bf16[32,32,512]{2,0,1:T(8,128)(2,1)}), bf16[32,32,512]{2,0,1:T(8,128)(2,1)S(1)}, u32[]{:S(2)}, u32[]{:S(2)}) async-start(bf16[32,32,512]{2,0,1:T(8,128)(2,1)} %bitcast.15), calls=%async_computation | async-start | bytes 2097152 | tf_op jit(solution)/shard_map/all_to_all | solution.py:173
  35.2 5.9 %collective-permute-start = (bf16[1040,128]{1,0:T(8,128)(2,1)S(1)}, bf16[1040,128]{1,0:T(8,128)(2,1)S(1)}, u32[]{:S(2)}, u32[]{:S(2)}) collective-permute-start(bf16[1040,128]{1,0:T(8,128)(2,1)S(1)} %get-tuple-element.7.tail_ref), channel_id=1, source_target_pairs={{0,1},{1,2},{2,3},{3,4},{4,5},{5,6},{6,7},{7,8},{8,9},{9,10},{10,1... | collective-permute-start | bytes 798728 | tf_op jit(solution)/shard_map/ppermute | solution.py:182
  35.2 5.8 %collective-permute-start.1 = (bf16[1040,128]{1,0:T(8,128)(2,1)S(1)}, bf16[1040,128]{1,0:T(8,128)(2,1)S(1)}, u32[]{:S(2)}, u32[]{:S(2)}) collective-permute-start(bf16[1040,128]{1,0:T(8,128)(2,1)S(1)} %get-tuple-element.8.head_ref), channel_id=1, source_target_pairs={{1,0},{2,1},{3,2},{4,3},{5,4},{6,5},{7,6},{8,7},{9,8},{10,9},{11,1... | collective-permute-start | bytes 798728 | tf_op jit(solution)/shard_map/ppermute | solution.py:183

commit v5 on v4

--- a/solution.py
+++ b/solution.py
@@ -11,6 +11,7 @@
 DEGREE = 7
 NODES = DEGREE + 1
 PAD = 16
+GROUP = 8
 
 
 def tables():
@@ -122,21 +123,22 @@
         out_ref[block, :] = (state_ref[block, :].astype(jnp.float32) + shift + update).astype(jnp.bfloat16)
 
 
-def gather_kernel(array_ref, out_ref, done):
-    count, _, width = out_ref.shape
-    copies = [
-        pltpu.make_async_copy(array_ref.at[:, pl.ds(k * width, width)], out_ref.at[k], done.at[k])
-        for k in range(count)
-    ]
-    for copy in copies:
+def gather_kernel(array_ref, out_ref, held, came, left):
+    count = array_ref.shape[0]
+    inward = [pltpu.make_async_copy(array_ref.at[k], held.at[k], came.at[k]) for k in range(count)]
+    outward = [pltpu.make_async_copy(held.at[k], out_ref.at[:, k], left.at[k]) for k in range(count)]
+    for copy in inward:
         copy.start()
-    for copy in copies:
+    for arrived, copy in zip(inward, outward):
+        arrived.wait()
+        copy.start()
+    for copy in outward:
         copy.wait()
 
 
 VMEM = pl.BlockSpec(memory_space=pltpu.VMEM)
 SMEM = pl.BlockSpec(memory_space=pltpu.SMEM)
-ANY = pl.BlockSpec(memory_space=pl.ANY)
+HBM = pl.BlockSpec(memory_space=pltpu.HBM)
 
 
 def struct(shape):
@@ -164,13 +166,21 @@
     half = own // 2
     bf16 = jnp.bfloat16
 
-    blocks = call(
-        gather_kernel, (obs_ens,), [VMEM], (bf16, devices, share, own), ANY,
-        [pltpu.SemaphoreType.DMA((devices,))],
-    )
-    region_obs = lax.all_to_all(blocks, "mem", split_axis=0, concat_axis=0, tiled=True)
-    region_obs = region_obs.reshape(devices * share, own)
-    region_state = lax.all_to_all(state, "mem", split_axis=1, concat_axis=0, tiled=True)
+    groups = share // GROUP
+
+    def exchanged(array):
+        width = array.shape[1] // devices
+        tiles = array.reshape(groups, GROUP, devices, width).transpose(0, 2, 1, 3)
+        blocks = call(
+            gather_kernel, (pltpu.with_memory_space_constraint(tiles, pltpu.HBM),), [HBM],
+            (bf16, devices, groups, GROUP, width), HBM,
+            [pltpu.VMEM(tiles.shape, bf16), pltpu.SemaphoreType.DMA((groups,)), pltpu.SemaphoreType.DMA((groups,))],
+        )
+        arrived = lax.all_to_all(blocks, "mem", split_axis=0, concat_axis=0, tiled=True)
+        return arrived.reshape(devices * share, width)
+
+    region_obs = exchanged(obs_ens)
+    region_state = exchanged(state)
     members, columns = region_state.shape
 
     edge = (bf16, members + PAD, half)

time: 96.9 us -> 96.6 us (level)
  the two profiles are of different devices: /device:TPU:322 before, /device:TPU:578 now
where the time goes in v5:
time: 96.6 us; the launch traced here: 96.2 us
  blocking collectives  32.1 us (33%)
  waiting for transfers between devices  31.4 us (33%)
  starting transfers between devices  17.6 us (18%)
  Pallas kernels  14 us (14%)
  local copies, waits for them, and re-layouts  1.09 us (1%)
    all_to_all x1, blocking collectives, on_device(): lax.all_to_all(analysed, 'mem', split_axis=0, concat_axis=1, tiled=True)  32.1 us
    all_to_all x2, waiting for transfers between devices, exchanged(): lax.all_to_all(blocks, 'mem', split_axis=0, concat_axis=0, tiled=True)  27.3 us
    all_to_all x2, starting transfers between devices, exchanged(): lax.all_to_all(blocks, 'mem', split_axis=0, concat_axis=0, tiled=True)  15.8 us
    pallas_call x5, Pallas kernels, call(): pl.pallas_call(kernel, out_shape=jax.tree.map(struct, outs, is_leaf=lambd...  14 us
    ppermute x1, waiting for transfers between devices, on_device(): lax.ppermute(tail, 'patch', [(i, (i + 1) % patches) for i in range(patche...  4.09 us
  transfers between devices with their start and end apart: 4, of which 3 were waited for; matrix products, arithmetic and copies ran while one was open for 0% of the time, Pallas kernels for 11%

profile of v5, /device:TPU:578, one launch (start us, length us, event | category | flops | bytes accessed | tf_op | source)
XLA Modules:
  0.0 96.2 jit_solution(1782767998097857316)
XLA Ops:
  0.0 1.8 %shard_map.65 = bf16[32,4,8,256]{3,2,1,0:T(8,128)(2,1)} custom-call(bf16[4,32,8,256]{3,2,1,0:T(8,128)(2,1)} %bitcast.24), custom_call_target="tpu_custom_call" | custom-call | flops 1000000 | bytes 1000000 | tf_op jit(solution)/shard_map/pallas_call | solution.py:149
  1.9 10.3 %all-to-all-start.1 = ((bf16[32,4,8,256]{3,2,1,0:T(8,128)(2,1)}), bf16[32,4,8,256]{3,2,1,0:T(8,128)(2,1)S(1)}, u32[]{:S(2)}, u32[]{:S(2)}) async-start(bf16[32,4,8,256]{3,2,1,0:T(8,128)(2,1)} %shard_map.65), calls=%async_computation.1 | async-start | bytes 1048576 | tf_op jit(solution)/shard_map/all_to_all | solution.py:179
  12.1 0.0 copy-start
  12.1 0.0 copy-start.1
  12.1 0.0 copy-start.2
  12.2 0.0 copy-start.3
  12.2 2.0 %shard_map.64 = bf16[32,4,8,512]{3,2,1,0:T(8,128)(2,1)} custom-call(bf16[4,32,8,512]{3,2,1,0:T(8,128)(2,1)} %bitcast.23), custom_call_target="tpu_custom_call" | custom-call | flops 1000000 | bytes 1000000 | tf_op jit(solution)/shard_map/pallas_call | solution.py:149
  14.2 14.8 %all-to-all-done.1 = bf16[32,4,8,256]{3,2,1,0:T(8,128)(2,1)S(1)} async-done(((bf16[32,4,8,256]{3,2,1,0:T(8,128)(2,1)}), bf16[32,4,8,256]{3,2,1,0:T(8,128)(2,1)S(1)}, u32[]{:S(2)}, u32[]{:S(2)}) %all-to-all-start.1) | async-done | bytes 524320 | tf_op jit(solution)/shard_map/all_to_all | solution.py:179
  29.0 5.6 %all-to-all-start = ((bf16[32,4,8,512]{3,2,1,0:T(8,128)(2,1)}), bf16[32,4,8,512]{3,2,1,0:T(8,128)(2,1)S(1)}, u32[]{:S(2)}, u32[]{:S(2)}) async-start(bf16[32,4,8,512]{3,2,1,0:T(8,128)(2,1)} %shard_map.64), calls=%async_computation | async-start | bytes 2097152 | tf_op jit(solution)/shard_map/all_to_all | solution.py:179
  34.5 0.0 copy-done
  34.5 0.0 copy-done.1
  34.6 0.0 copy-done.2
  34.6 0.3 shard_map.66
  34.9 0.0 collective-permute-start
  34.9 1.7 %collective-permute-start.1 = (bf16[1040,128]{1,0:T(8,128)(2,1)S(1)}, bf16[1040,128]{1,0:T(8,128)(2,1)S(1)}, u32[]{:S(2)}, u32[]{:S(2)}) collective-permute-start(bf16[1040,128]{1,0:T(8,128)(2,1)S(1)} %get-tuple-element.8.head_ref), channel_id=1, source_target_pairs={{1,0},{2,1},{3,2},{4,3},{5,4},{6,5},{7,6},{8,7},{9,8},{10,9},{11,1... | collective-permute-start | bytes 798728 | tf_op jit(solution)/shard_map/ppermute | solution.py:193
  36.7 4.1 %collective-permute-done.left_ref = bf16[1040,128]{1,0:T(8,128)(2,1)S(1)} collective-permute-done((bf16[1040,128]{1,0:T(8,128)(2,1)S(1)}, bf16[1040,128]{1,0:T(8,128)(2,1)S(1)}, u32[]{:S(2)}, u32[]{:S(2)}) %collective-permute-start) | collective-permute-done | bytes 266272 | tf_op jit(solution)/shard_map/ppermute | solution.py:192
  40.8 0.0 collective-permute-done.1.right_ref
  40.8 0.0 copy-done.3
  40.8 8.4 %shard_map.67.weights_ref = bf16[1040,1024]{1,0:T(8,128)(2,1)S(1)} custom-call(bf16[1040,128]{1,0:T(8,128)(2,1)S(1)} %collective-permute-done.left_ref, bf16[1040,128]{1,0:T(8,128)(2,1)S(1)} %get-tuple-element.8.head_ref, bf16[1040,128]{1,0:T(8,128)(2,1)S(1)} %get-tuple-element.7.tail_ref, bf16[1040,128]{1,0:T(8,128)(2,1)S(1)} %collective-permute-done.1.right_ref, ...), custom_call_target="tpu_custom_call" | custom-call | flops 7000000000 | bytes 4000000 | tf_op jit(solution)/shard_map/pallas_call | solution.py:149
  49.2 12.5 %all-to-all-done = bf16[32,4,8,512]{3,2,1,0:T(8,128)(2,1)S(1)} async-done(((bf16[32,4,8,512]{3,2,1,0:T(8,128)(2,1)}), bf16[32,4,8,512]{3,2,1,0:T(8,128)(2,1)S(1)}, u32[]{:S(2)}, u32[]{:S(2)}) %all-to-all-start) | async-done | bytes 1048608 | tf_op jit(solution)/shard_map/all_to_all | solution.py:179
  61.7 1.4 %shard_map.68 = bf16[1024,512]{1,0:T(8,128)(2,1)S(1)} custom-call(bf16[1024,512]{1,0:T(8,128)(2,1)S(1)} %bitcast.16, bf16[1040,1024]{1,0:T(8,128)(2,1)S(1)} %shard_map.67.weights_ref), custom_call_target="tpu_custom_call" | custom-call | flops 1000000000 | bytes 4000000 | tf_op jit(solution)/shard_map/pallas_call | solution.py:149
  63.1 32.1 %all_to_all.29 = bf16[32,32,512]{2,1,0:T(8,128)(2,1)S(1)} all-to-all(bf16[32,32,512]{2,1,0:T(8,128)(2,1)S(1)} %bitcast.17), channel_id=1, replica_groups=mesh['mem'=32,'patch'=24] {'mem'}, dimensions={0} | all-to-all | bytes 2097152 | tf_op jit(solution)/shard_map/all_to_all | solution.py:204
  95.1 1.1 %copy.8 = bf16[32,4,8,512]{3,2,0,1:T(8,128)(2,1)} copy(bf16[32,4,8,512]{3,2,1,0:T(8,128)(2,1)S(1)} %bitcast.22) | data formatting | bytes 2097152 | tf_op jit(solution)/shard_map/all_to_all | solution.py:204
Async XLA Ops:
  1.9 27.1 %all-to-all-start.1 = ((bf16[32,4,8,256]{3,2,1,0:T(8,128)(2,1)}), bf16[32,4,8,256]{3,2,1,0:T(8,128)(2,1)S(1)}, u32[]{:S(2)}, u32[]{:S(2)}) async-start(bf16[32,4,8,256]{3,2,1,0:T(8,128)(2,1)} %shard_map.65), calls=%async_computation.1 | async-start | bytes 1048576 | tf_op jit(solution)/shard_map/all_to_all | solution.py:179
  12.1 22.4 %copy-start = (f32[8192]{0:T(1024)S(1)}, f32[8192]{0:T(1024)}, u32[]{:S(2)}) copy-start(f32[8192]{0:T(1024)} %param.8) | copy-start | bytes 98308
  12.1 22.4 %copy-start.1 = (f32[8192]{0:T(1024)S(1)}, f32[8192]{0:T(1024)}, u32[]{:S(2)}) copy-start(f32[8192]{0:T(1024)} %param.9) | copy-start | bytes 98308
  12.1 22.4 %copy-start.2 = (s32[32]{0:T(128)S(1)}, s32[32]{0:T(128)}, u32[]{:S(2)}) copy-start(s32[32]{0:T(128)} %param.10) | copy-start | bytes 388
  12.2 28.6 %copy-start.3 = (f32[16,128]{1,0:T(8,128)S(1)}, f32[16,128]{1,0:T(8,128)}, u32[]{:S(2)}) copy-start(f32[16,128]{1,0:T(8,128)} %constant.7.clone.table_ref) | copy-start | bytes 24580
  29.0 32.7 %all-to-all-start = ((bf16[32,4,8,512]{3,2,1,0:T(8,128)(2,1)}), bf16[32,4,8,512]{3,2,1,0:T(8,128)(2,1)S(1)}, u32[]{:S(2)}, u32[]{:S(2)}) async-start(bf16[32,4,8,512]{3,2,1,0:T(8,128)(2,1)} %shard_map.64), calls=%async_computation | async-start | bytes 2097152 | tf_op jit(solution)/shard_map/all_to_all | solution.py:179
  34.9 5.9 %collective-permute-start = (bf16[1040,128]{1,0:T(8,128)(2,1)S(1)}, bf16[1040,128]{1,0:T(8,128)(2,1)S(1)}, u32[]{:S(2)}, u32[]{:S(2)}) collective-permute-start(bf16[1040,128]{1,0:T(8,128)(2,1)S(1)} %get-tuple-element.7.tail_ref), channel_id=1, source_target_pairs={{0,1},{1,2},{2,3},{3,4},{4,5},{5,6},{6,7},{7,8},{8,9},{9,10},{10,1... | collective-permute-start | bytes 798728 | tf_op jit(solution)/shard_map/ppermute | solution.py:192
  34.9 5.8 %collective-permute-start.1 = (bf16[1040,128]{1,0:T(8,128)(2,1)S(1)}, bf16[1040,128]{1,0:T(8,128)(2,1)S(1)}, u32[]{:S(2)}, u32[]{:S(2)}) collective-permute-start(bf16[1040,128]{1,0:T(8,128)(2,1)S(1)} %get-tuple-element.8.head_ref), channel_id=1, source_target_pairs={{1,0},{2,1},{3,2},{4,3},{5,4},{6,5},{7,6},{8,7},{9,8},{10,9},{11,1... | collective-permute-start | bytes 798728 | tf_op jit(solution)/shard_map/ppermute | solution.py:193

commit v6 on v5

--- a/solution.py
+++ b/solution.py
@@ -55,17 +55,35 @@
         out[members:, :] = jnp.broadcast_to(innov, (PAD, half)).astype(jnp.bfloat16)
 
 
-def weights_kernel(left_ref, head_ref, tail_ref, right_ref, table_ref, out_ref, gains, turned):
+def own_kernel(head_ref, tail_ref, gains_ref, turned_ref, inner_ref):
+    members, own = gains_ref.shape
+    half = own // 2
+    for part, ref in enumerate((head_ref, tail_ref)):
+        block = ref[0:members, :]
+        gains_ref[:, part * half : (part + 1) * half] = block
+        turned_ref[part * half : (part + 1) * half, :] = block.T
+    inner_ref[...] = dot(turned_ref[...], gains_ref[...])
+
+
+def weights_kernel(
+    left_ref, head_ref, tail_ref, right_ref, table_ref, own_ref, own_turned_ref, inner_ref, out_ref, gains, turned
+):
     members, sites = gains.shape
     half = sites // 4
-    parts = (left_ref, head_ref, tail_ref, right_ref)
-    for part, ref in enumerate(parts):
+    own = 2 * half
+    parts = (head_ref, tail_ref, left_ref, right_ref)
+    gains[:, :own] = own_ref[...]
+    turned[:own, :] = own_turned_ref[...]
+    for part, ref in ((2, left_ref), (3, right_ref)):
         block = ref[0:members, :]
         gains[:, part * half : (part + 1) * half] = block
         turned[part * half : (part + 1) * half, :] = block.T
     innov = jnp.concatenate([ref[members:, :] for ref in parts], axis=1)
 
-    normal = dot(turned[...], gains[...]) * (1.0 / (members - 1))
+    inner = inner_ref[...]
+    edge = dot(turned[own:, :], gains[...])
+    cross = edge[:, :own]
+    normal = jnp.concatenate([jnp.concatenate([inner, cross.T], axis=1), edge], axis=0) * (1.0 / (members - 1))
     upper = jnp.max(jnp.sum(jnp.abs(normal), axis=0, keepdims=True), axis=1, keepdims=True) + 1e-06
     nodes = upper * table_ref[NODES : NODES + 1, :]
     lifted = jnp.sqrt(1.0 + nodes)
@@ -114,13 +132,13 @@
 
 def apply_kernel(state_ref, weights_ref, out_ref):
     members = state_ref.shape[0]
-    below = dot(weights_ref[members:, :], state_ref[...])
+    last = members - 128
+    below = dot(weights_ref[last:, :], state_ref[...])
+    update, below = below[: members - last, :], below[members - last :, :]
     shift = below[0:1, :] + below[PAD // 2 : PAD // 2 + 1, :]
-    step = 256
-    for start in range(0, members, step):
-        block = slice(start, start + step)
-        update = dot(weights_ref[block, :], state_ref[...])
-        out_ref[block, :] = (state_ref[block, :].astype(jnp.float32) + shift + update).astype(jnp.bfloat16)
+    out_ref[last:members, :] = (state_ref[last:members, :].astype(jnp.float32) + shift + update).astype(jnp.bfloat16)
+    update = dot(weights_ref[:last, :], state_ref[...])
+    out_ref[:last, :] = (state_ref[:last, :].astype(jnp.float32) + shift + update).astype(jnp.bfloat16)
 
 
 def gather_kernel(array_ref, out_ref, held, came, left):
@@ -191,8 +209,12 @@
     )
     left = lax.ppermute(tail, "patch", [(i, (i + 1) % patches) for i in range(patches)])
     right = lax.ppermute(head, "patch", [((i + 1) % patches, i) for i in range(patches)])
+    own_parts = call(
+        own_kernel, (head, tail), [VMEM] * 2,
+        [(bf16, members, own), (bf16, own, members), (jnp.float32, own, own)], [VMEM] * 3,
+    )
     transform = call(
-        weights_kernel, (left, head, tail, right, jnp.asarray(tables())), [VMEM] * 5,
+        weights_kernel, (left, head, tail, right, jnp.asarray(tables()), *own_parts), [VMEM] * 8,
         (bf16, members + PAD, members), VMEM,
         [pltpu.VMEM((members, 2 * own), bf16), pltpu.VMEM((2 * own, members), bf16)],
         7 * 10**9, 4 * 10**6, 24,

time: 96.6 us -> 96.5 us (level)
  the two profiles are of different devices: /device:TPU:578 before, /device:TPU:514 now
where the time goes in v6:
time: 96.5 us; the launch traced here: 96.1 us
  blocking collectives  32.1 us (33%)
  waiting for transfers between devices  30 us (31%)
  starting transfers between devices  18.8 us (19%)
  Pallas kernels  14 us (15%)
  local copies, waits for them, and re-layouts  1.09 us (1%)
    all_to_all x1, blocking collectives, on_device(): lax.all_to_all(analysed, 'mem', split_axis=0, concat_axis=1, tiled=True)  32.1 us
    all_to_all x2, waiting for transfers between devices, exchanged(): lax.all_to_all(blocks, 'mem', split_axis=0, concat_axis=0, tiled=True)  26.3 us
    all_to_all x2, starting transfers between devices, exchanged(): lax.all_to_all(blocks, 'mem', split_axis=0, concat_axis=0, tiled=True)  15.8 us
    pallas_call x6, Pallas kernels, call(): pl.pallas_call(kernel, out_shape=jax.tree.map(struct, outs, is_leaf=lambd...  14 us
    ppermute x1, waiting for transfers between devices, on_device(): lax.ppermute(tail, 'patch', [(i, (i + 1) % patches) for i in range(patche...  3.72 us
    ppermute x1, starting transfers between devices, on_device(): lax.ppermute(head, 'patch', [((i + 1) % patches, i) for i in range(patche...  2.94 us
  transfers between devices with their start and end apart: 4, of which 3 were waited for; matrix products, arithmetic and copies ran while one was open for 0% of the time, Pallas kernels for 11%

profile of v6, /device:TPU:514, one launch (start us, length us, event | category | flops | bytes accessed | tf_op | source)
XLA Modules:
  0.0 96.1 jit_solution(3056195086271376169)
XLA Ops:
  0.0 1.8 %shard_map.65 = bf16[32,4,8,256]{3,2,1,0:T(8,128)(2,1)} custom-call(bf16[4,32,8,256]{3,2,1,0:T(8,128)(2,1)} %bitcast.24), custom_call_target="tpu_custom_call" | custom-call | flops 1000000 | bytes 1000000 | tf_op jit(solution)/shard_map/pallas_call | solution.py:167
  1.8 10.3 %all-to-all-start.1 = ((bf16[32,4,8,256]{3,2,1,0:T(8,128)(2,1)}), bf16[32,4,8,256]{3,2,1,0:T(8,128)(2,1)S(1)}, u32[]{:S(2)}, u32[]{:S(2)}) async-start(bf16[32,4,8,256]{3,2,1,0:T(8,128)(2,1)} %shard_map.65), calls=%async_computation.1 | async-start | bytes 1048576 | tf_op jit(solution)/shard_map/all_to_all | solution.py:197
  12.1 0.0 copy-start
  12.1 0.0 copy-start.1
  12.1 0.0 copy-start.2
  12.2 2.0 %shard_map.64 = bf16[32,4,8,512]{3,2,1,0:T(8,128)(2,1)} custom-call(bf16[4,32,8,512]{3,2,1,0:T(8,128)(2,1)} %bitcast.23), custom_call_target="tpu_custom_call" | custom-call | flops 1000000 | bytes 1000000 | tf_op jit(solution)/shard_map/pallas_call | solution.py:167
  14.2 0.0 copy-start.3
  14.2 14.8 %all-to-all-done.1 = bf16[32,4,8,256]{3,2,1,0:T(8,128)(2,1)S(1)} async-done(((bf16[32,4,8,256]{3,2,1,0:T(8,128)(2,1)}), bf16[32,4,8,256]{3,2,1,0:T(8,128)(2,1)S(1)}, u32[]{:S(2)}, u32[]{:S(2)}) %all-to-all-start.1) | async-done | bytes 524320 | tf_op jit(solution)/shard_map/all_to_all | solution.py:197
  28.9 5.6 %all-to-all-start = ((bf16[32,4,8,512]{3,2,1,0:T(8,128)(2,1)}), bf16[32,4,8,512]{3,2,1,0:T(8,128)(2,1)S(1)}, u32[]{:S(2)}, u32[]{:S(2)}) async-start(bf16[32,4,8,512]{3,2,1,0:T(8,128)(2,1)} %shard_map.64), calls=%async_computation | async-start | bytes 2097152 | tf_op jit(solution)/shard_map/all_to_all | solution.py:197
  34.5 0.0 copy-done
  34.5 0.0 copy-done.1
  34.5 0.0 copy-done.2
  34.6 0.3 shard_map.66
  34.9 0.0 collective-permute-start
  34.9 2.9 %collective-permute-start.1 = (bf16[1040,128]{1,0:T(8,128)(2,1)S(1)}, bf16[1040,128]{1,0:T(8,128)(2,1)S(1)}, u32[]{:S(2)}, u32[]{:S(2)}) collective-permute-start(bf16[1040,128]{1,0:T(8,128)(2,1)S(1)} %get-tuple-element.11.head_ref), channel_id=1, source_target_pairs={{1,0},{2,1},{3,2},{4,3},{5,4},{6,5},{7,6},{8,7},{9,8},{10,9},{11,1... | collective-permute-start | bytes 798728 | tf_op jit(solution)/shard_map/ppermute | solution.py:211
  37.9 0.4 shard_map.67
  38.3 3.7 %collective-permute-done.left_ref = bf16[1040,128]{1,0:T(8,128)(2,1)S(1)} collective-permute-done((bf16[1040,128]{1,0:T(8,128)(2,1)S(1)}, bf16[1040,128]{1,0:T(8,128)(2,1)S(1)}, u32[]{:S(2)}, u32[]{:S(2)}) %collective-permute-start) | collective-permute-done | bytes 266272 | tf_op jit(solution)/shard_map/ppermute | solution.py:210
  42.0 0.0 collective-permute-done.1.right_ref
  42.0 0.0 copy-done.3
  42.0 8.2 %shard_map.68.weights_ref = bf16[1040,1024]{1,0:T(8,128)(2,1)S(1)} custom-call(bf16[1040,128]{1,0:T(8,128)(2,1)S(1)} %collective-permute-done.left_ref, bf16[1040,128]{1,0:T(8,128)(2,1)S(1)} %get-tuple-element.11.head_ref, bf16[1040,128]{1,0:T(8,128)(2,1)S(1)} %get-tuple-element.10.tail_ref, bf16[1040,128]{1,0:T(8,128)(2,1)S(1)} %collective-permute-done.1.right_ref, ...), custom_call_target="tpu_custom_call" | custom-call | flops 7000000000 | bytes 4000000 | tf_op jit(solution)/shard_map/pallas_call | solution.py:167
  50.2 11.5 %all-to-all-done = bf16[32,4,8,512]{3,2,1,0:T(8,128)(2,1)S(1)} async-done(((bf16[32,4,8,512]{3,2,1,0:T(8,128)(2,1)}), bf16[32,4,8,512]{3,2,1,0:T(8,128)(2,1)S(1)}, u32[]{:S(2)}, u32[]{:S(2)}) %all-to-all-start) | async-done | bytes 1048608 | tf_op jit(solution)/shard_map/all_to_all | solution.py:197
  61.7 1.3 %shard_map.69 = bf16[1024,512]{1,0:T(8,128)(2,1)S(1)} custom-call(bf16[1024,512]{1,0:T(8,128)(2,1)S(1)} %bitcast.16, bf16[1040,1024]{1,0:T(8,128)(2,1)S(1)} %shard_map.68.weights_ref), custom_call_target="tpu_custom_call" | custom-call | flops 1000000000 | bytes 4000000 | tf_op jit(solution)/shard_map/pallas_call | solution.py:167
  63.0 32.1 %all_to_all.29 = bf16[32,32,512]{2,1,0:T(8,128)(2,1)S(1)} all-to-all(bf16[32,32,512]{2,1,0:T(8,128)(2,1)S(1)} %bitcast.17), channel_id=1, replica_groups=mesh['mem'=32,'patch'=24] {'mem'}, dimensions={0} | all-to-all | bytes 2097152 | tf_op jit(solution)/shard_map/all_to_all | solution.py:226
  95.0 1.1 %copy.8 = bf16[32,4,8,512]{3,2,0,1:T(8,128)(2,1)} copy(bf16[32,4,8,512]{3,2,1,0:T(8,128)(2,1)S(1)} %bitcast.22) | data formatting | bytes 2097152 | tf_op jit(solution)/shard_map/all_to_all | solution.py:226
Async XLA Ops:
  1.8 27.1 %all-to-all-start.1 = ((bf16[32,4,8,256]{3,2,1,0:T(8,128)(2,1)}), bf16[32,4,8,256]{3,2,1,0:T(8,128)(2,1)S(1)}, u32[]{:S(2)}, u32[]{:S(2)}) async-start(bf16[32,4,8,256]{3,2,1,0:T(8,128)(2,1)} %shard_map.65), calls=%async_computation.1 | async-start | bytes 1048576 | tf_op jit(solution)/shard_map/all_to_all | solution.py:197
  12.1 22.4 %copy-start = (f32[8192]{0:T(1024)S(1)}, f32[8192]{0:T(1024)}, u32[]{:S(2)}) copy-start(f32[8192]{0:T(1024)} %param.8) | copy-start | bytes 98308
  12.1 22.4 %copy-start.1 = (f32[8192]{0:T(1024)S(1)}, f32[8192]{0:T(1024)}, u32[]{:S(2)}) copy-start(f32[8192]{0:T(1024)} %param.9) | copy-start | bytes 98308
  12.1 22.4 %copy-start.2 = (s32[32]{0:T(128)S(1)}, s32[32]{0:T(128)}, u32[]{:S(2)}) copy-start(s32[32]{0:T(128)} %param.10) | copy-start | bytes 388
  14.2 27.8 %copy-start.3 = (f32[16,128]{1,0:T(8,128)S(1)}, f32[16,128]{1,0:T(8,128)}, u32[]{:S(2)}) copy-start(f32[16,128]{1,0:T(8,128)} %constant.7.clone.table_ref) | copy-start | bytes 24580
  28.9 32.7 %all-to-all-start = ((bf16[32,4,8,512]{3,2,1,0:T(8,128)(2,1)}), bf16[32,4,8,512]{3,2,1,0:T(8,128)(2,1)S(1)}, u32[]{:S(2)}, u32[]{:S(2)}) async-start(bf16[32,4,8,512]{3,2,1,0:T(8,128)(2,1)} %shard_map.64), calls=%async_computation | async-start | bytes 2097152 | tf_op jit(solution)/shard_map/all_to_all | solution.py:197
  34.9 7.1 %collective-permute-start = (bf16[1040,128]{1,0:T(8,128)(2,1)S(1)}, bf16[1040,128]{1,0:T(8,128)(2,1)S(1)}, u32[]{:S(2)}, u32[]{:S(2)}) collective-permute-start(bf16[1040,128]{1,0:T(8,128)(2,1)S(1)} %get-tuple-element.10.tail_ref), channel_id=1, source_target_pairs={{0,1},{1,2},{2,3},{3,4},{4,5},{5,6},{6,7},{7,8},{8,9},{9,10},{10,1... | collective-permute-start | bytes 798728 | tf_op jit(solution)/shard_map/ppermute | solution.py:210
  34.9 7.0 %collective-permute-start.1 = (bf16[1040,128]{1,0:T(8,128)(2,1)S(1)}, bf16[1040,128]{1,0:T(8,128)(2,1)S(1)}, u32[]{:S(2)}, u32[]{:S(2)}) collective-permute-start(bf16[1040,128]{1,0:T(8,128)(2,1)S(1)} %get-tuple-element.11.head_ref), channel_id=1, source_target_pairs={{1,0},{2,1},{3,2},{4,3},{5,4},{6,5},{7,6},{8,7},{9,8},{10,9},{11,1... | collective-permute-start | bytes 798728 | tf_op jit(solution)/shard_map/ppermute | solution.py:211

commit v7 on v6

--- a/solution.py
+++ b/solution.py
@@ -154,6 +154,21 @@
         copy.wait()
 
 
+def scatter_kernel(blocks_ref, out_ref, done):
+    count, half = out_ref.shape[0], out_ref.shape[1] // 2
+    copies = [
+        pltpu.make_async_copy(
+            blocks_ref.at[pl.ds(part * half, half), k], out_ref.at[k, pl.ds(part * half, half)], done.at[2 * k + part]
+        )
+        for k in range(count)
+        for part in range(2)
+    ]
+    for copy in copies:
+        copy.start()
+    for copy in copies:
+        copy.wait()
+
+
 VMEM = pl.BlockSpec(memory_space=pltpu.VMEM)
 SMEM = pl.BlockSpec(memory_space=pltpu.SMEM)
 HBM = pl.BlockSpec(memory_space=pltpu.HBM)
@@ -223,7 +238,14 @@
         apply_kernel, (region_state, transform), [VMEM] * 2, (bf16, members, columns), VMEM,
         (), 10**9, 4 * 10**6, 8,
     )
-    return lax.all_to_all(analysed, "mem", split_axis=0, concat_axis=1, tiled=True)
+    returned = lax.all_to_all(
+        analysed.reshape(devices, groups, GROUP, columns), "mem", split_axis=0, concat_axis=0, tiled=True
+    )
+    tiles = call(
+        scatter_kernel, (returned,), [VMEM], (bf16, groups, devices, GROUP, columns), HBM,
+        [pltpu.SemaphoreType.DMA((2 * groups,))],
+    )
+    return tiles.transpose(0, 2, 1, 3).reshape(share, devices * columns)
 
 
 def solution(mesh):

time: 96.5 us -> 96.4 us (level)
  the two profiles are of different devices: /device:TPU:514 before, /device:TPU:450 now
where the time goes in v7:
time: 96.4 us; the launch traced here: 96.1 us
  blocking collectives  32.1 us (33%)
  waiting for transfers between devices  31.2 us (32%)
  starting transfers between devices  17.6 us (18%)
  Pallas kernels  15 us (16%)
    all_to_all x1, blocking collectives, on_device(): lax.all_to_all(analysed.reshape(devices, groups, GROUP, columns), 'mem',...  32.1 us
    all_to_all x2, waiting for transfers between devices, exchanged(): lax.all_to_all(blocks, 'mem', split_axis=0, concat_axis=0, tiled=True)  27.5 us
    all_to_all x2, starting transfers between devices, exchanged(): lax.all_to_all(blocks, 'mem', split_axis=0, concat_axis=0, tiled=True)  15.8 us
    pallas_call x7, Pallas kernels, call(): pl.pallas_call(kernel, out_shape=jax.tree.map(struct, outs, is_leaf=lambd...  15 us
    ppermute x1, waiting for transfers between devices, on_device(): lax.ppermute(tail, 'patch', [(i, (i + 1) % patches) for i in range(patche...  3.72 us
  transfers between devices with their start and end apart: 4, of which 3 were waited for; matrix products, arithmetic and copies ran while one was open for 0% of the time, Pallas kernels for 11%

profile of v7, /device:TPU:450, one launch (start us, length us, event | category | flops | bytes accessed | tf_op | source)
XLA Modules:
  0.0 96.1 jit_solution(17147516169285279685)
XLA Ops:
  0.0 1.8 %shard_map.65 = bf16[32,4,8,256]{3,2,1,0:T(8,128)(2,1)} custom-call(bf16[4,32,8,256]{3,2,1,0:T(8,128)(2,1)} %bitcast.23), custom_call_target="tpu_custom_call" | custom-call | flops 1000000 | bytes 1000000 | tf_op jit(solution)/shard_map/pallas_call | solution.py:182
  1.8 10.3 %all-to-all-start.1 = ((bf16[32,4,8,256]{3,2,1,0:T(8,128)(2,1)}), bf16[32,4,8,256]{3,2,1,0:T(8,128)(2,1)S(1)}, u32[]{:S(2)}, u32[]{:S(2)}) async-start(bf16[32,4,8,256]{3,2,1,0:T(8,128)(2,1)} %shard_map.65), calls=%async_computation.1 | async-start | bytes 1048576 | tf_op jit(solution)/shard_map/all_to_all | solution.py:212
  12.1 0.0 copy-start
  12.1 0.0 copy-start.1
  12.1 0.0 copy-start.2
  12.2 2.0 %shard_map.64 = bf16[32,4,8,512]{3,2,1,0:T(8,128)(2,1)} custom-call(bf16[4,32,8,512]{3,2,1,0:T(8,128)(2,1)} %bitcast.22), custom_call_target="tpu_custom_call" | custom-call | flops 1000000 | bytes 1000000 | tf_op jit(solution)/shard_map/pallas_call | solution.py:182
  14.2 0.0 copy-start.3
  14.2 14.8 %all-to-all-done.1 = bf16[32,4,8,256]{3,2,1,0:T(8,128)(2,1)S(1)} async-done(((bf16[32,4,8,256]{3,2,1,0:T(8,128)(2,1)}), bf16[32,4,8,256]{3,2,1,0:T(8,128)(2,1)S(1)}, u32[]{:S(2)}, u32[]{:S(2)}) %all-to-all-start.1) | async-done | bytes 524320 | tf_op jit(solution)/shard_map/all_to_all | solution.py:212
  28.9 5.6 %all-to-all-start = ((bf16[32,4,8,512]{3,2,1,0:T(8,128)(2,1)}), bf16[32,4,8,512]{3,2,1,0:T(8,128)(2,1)S(1)}, u32[]{:S(2)}, u32[]{:S(2)}) async-start(bf16[32,4,8,512]{3,2,1,0:T(8,128)(2,1)} %shard_map.64), calls=%async_computation | async-start | bytes 2097152 | tf_op jit(solution)/shard_map/all_to_all | solution.py:212
  34.5 0.0 copy-done
  34.5 0.0 copy-done.1
  34.5 0.0 copy-done.2
  34.6 0.3 shard_map.66
  34.9 0.0 collective-permute-start
  34.9 1.7 %collective-permute-start.1 = (bf16[1040,128]{1,0:T(8,128)(2,1)S(1)}, bf16[1040,128]{1,0:T(8,128)(2,1)S(1)}, u32[]{:S(2)}, u32[]{:S(2)}) collective-permute-start(bf16[1040,128]{1,0:T(8,128)(2,1)S(1)} %get-tuple-element.11.head_ref), channel_id=1, source_target_pairs={{1,0},{2,1},{3,2},{4,3},{5,4},{6,5},{7,6},{8,7},{9,8},{10,9},{11,1... | collective-permute-start | bytes 798728 | tf_op jit(solution)/shard_map/ppermute | solution.py:226
  36.7 0.4 shard_map.67
  37.0 3.7 %collective-permute-done.left_ref = bf16[1040,128]{1,0:T(8,128)(2,1)S(1)} collective-permute-done((bf16[1040,128]{1,0:T(8,128)(2,1)S(1)}, bf16[1040,128]{1,0:T(8,128)(2,1)S(1)}, u32[]{:S(2)}, u32[]{:S(2)}) %collective-permute-start) | collective-permute-done | bytes 266272 | tf_op jit(solution)/shard_map/ppermute | solution.py:225
  40.8 0.0 collective-permute-done.1.right_ref
  40.8 0.0 copy-done.3
  40.8 8.2 %shard_map.68.weights_ref = bf16[1040,1024]{1,0:T(8,128)(2,1)S(1)} custom-call(bf16[1040,128]{1,0:T(8,128)(2,1)S(1)} %collective-permute-done.left_ref, bf16[1040,128]{1,0:T(8,128)(2,1)S(1)} %get-tuple-element.11.head_ref, bf16[1040,128]{1,0:T(8,128)(2,1)S(1)} %get-tuple-element.10.tail_ref, bf16[1040,128]{1,0:T(8,128)(2,1)S(1)} %collective-permute-done.1.right_ref, ...), custom_call_target="tpu_custom_call" | custom-call | flops 7000000000 | bytes 4000000 | tf_op jit(solution)/shard_map/pallas_call | solution.py:182
  48.9 12.7 %all-to-all-done = bf16[32,4,8,512]{3,2,1,0:T(8,128)(2,1)S(1)} async-done(((bf16[32,4,8,512]{3,2,1,0:T(8,128)(2,1)}), bf16[32,4,8,512]{3,2,1,0:T(8,128)(2,1)S(1)}, u32[]{:S(2)}, u32[]{:S(2)}) %all-to-all-start) | async-done | bytes 1048608 | tf_op jit(solution)/shard_map/all_to_all | solution.py:212
  61.7 1.3 %shard_map.69 = bf16[1024,512]{1,0:T(8,128)(2,1)S(1)} custom-call(bf16[1024,512]{1,0:T(8,128)(2,1)S(1)} %bitcast.16, bf16[1040,1024]{1,0:T(8,128)(2,1)S(1)} %shard_map.68.weights_ref), custom_call_target="tpu_custom_call" | custom-call | flops 1000000000 | bytes 4000000 | tf_op jit(solution)/shard_map/pallas_call | solution.py:182
  63.0 32.1 %all_to_all.15.blocks_ref = bf16[32,4,8,512]{3,2,1,0:T(8,128)(2,1)S(1)} all-to-all(bf16[32,4,8,512]{3,2,1,0:T(8,128)(2,1)S(1)} %bitcast.17), channel_id=1, replica_groups=mesh['mem'=32,'patch'=24] {'mem'}, dimensions={0} | all-to-all | bytes 2097152 | tf_op jit(solution)/shard_map/all_to_all | solution.py:241
  95.0 1.0 %shard_map.70 = bf16[4,32,8,512]{3,2,1,0:T(8,128)(2,1)} custom-call(bf16[32,4,8,512]{3,2,1,0:T(8,128)(2,1)S(1)} %all_to_all.15.blocks_ref), custom_call_target="tpu_custom_call" | custom-call | flops 1000000 | bytes 1000000 | tf_op jit(solution)/shard_map/pallas_call | solution.py:182
Async XLA Ops:
  1.8 27.1 %all-to-all-start.1 = ((bf16[32,4,8,256]{3,2,1,0:T(8,128)(2,1)}), bf16[32,4,8,256]{3,2,1,0:T(8,128)(2,1)S(1)}, u32[]{:S(2)}, u32[]{:S(2)}) async-start(bf16[32,4,8,256]{3,2,1,0:T(8,128)(2,1)} %shard_map.65), calls=%async_computation.1 | async-start | bytes 1048576 | tf_op jit(solution)/shard_map/all_to_all | solution.py:212
  12.1 22.4 %copy-start = (f32[8192]{0:T(1024)S(1)}, f32[8192]{0:T(1024)}, u32[]{:S(2)}) copy-start(f32[8192]{0:T(1024)} %param.8) | copy-start | bytes 98308
  12.1 22.4 %copy-start.1 = (f32[8192]{0:T(1024)S(1)}, f32[8192]{0:T(1024)}, u32[]{:S(2)}) copy-start(f32[8192]{0:T(1024)} %param.9) | copy-start | bytes 98308
  12.1 22.4 %copy-start.2 = (s32[32]{0:T(128)S(1)}, s32[32]{0:T(128)}, u32[]{:S(2)}) copy-start(s32[32]{0:T(128)} %param.10) | copy-start | bytes 388
  14.2 26.6 %copy-start.3 = (f32[16,128]{1,0:T(8,128)S(1)}, f32[16,128]{1,0:T(8,128)}, u32[]{:S(2)}) copy-start(f32[16,128]{1,0:T(8,128)} %constant.7.clone.table_ref) | copy-start | bytes 24580
  28.9 32.7 %all-to-all-start = ((bf16[32,4,8,512]{3,2,1,0:T(8,128)(2,1)}), bf16[32,4,8,512]{3,2,1,0:T(8,128)(2,1)S(1)}, u32[]{:S(2)}, u32[]{:S(2)}) async-start(bf16[32,4,8,512]{3,2,1,0:T(8,128)(2,1)} %shard_map.64), calls=%async_computation | async-start | bytes 2097152 | tf_op jit(solution)/shard_map/all_to_all | solution.py:212
  34.9 5.9 %collective-permute-start = (bf16[1040,128]{1,0:T(8,128)(2,1)S(1)}, bf16[1040,128]{1,0:T(8,128)(2,1)S(1)}, u32[]{:S(2)}, u32[]{:S(2)}) collective-permute-start(bf16[1040,128]{1,0:T(8,128)(2,1)S(1)} %get-tuple-element.10.tail_ref), channel_id=1, source_target_pairs={{0,1},{1,2},{2,3},{3,4},{4,5},{5,6},{6,7},{7,8},{8,9},{9,10},{10,1... | collective-permute-start | bytes 798728 | tf_op jit(solution)/shard_map/ppermute | solution.py:225
  34.9 5.8 %collective-permute-start.1 = (bf16[1040,128]{1,0:T(8,128)(2,1)S(1)}, bf16[1040,128]{1,0:T(8,128)(2,1)S(1)}, u32[]{:S(2)}, u32[]{:S(2)}) collective-permute-start(bf16[1040,128]{1,0:T(8,128)(2,1)S(1)} %get-tuple-element.11.head_ref), channel_id=1, source_target_pairs={{1,0},{2,1},{3,2},{4,3},{5,4},{6,5},{7,6},{8,7},{9,8},{10,9},{11,1... | collective-permute-start | bytes 798728 | tf_op jit(solution)/shard_map/ppermute | solution.py:226
